TPU v7x, 32 devices: a whole 2x2x4 slice. The times are simulated.
32 devices in a mesh: leaf: 4 (over y, core), front: 8 (over z, x).
Axes of the slice: x: 2, y: 2, z: 4, core: 2. Of those that a mesh axis runs over, the one named last changes fastest.
Arguments:
- front_entries: float32 [8, 4, 128, 4, 8, 128], P(None, 'leaf', None, None, 'front'), as said below
- child_panels: bfloat16 [4, 1024, 512], P('leaf', 'front'), may hold values from -0.053955078 to 0.053955078
- child_blocks: bfloat16 [4, 1024, 1024], P('leaf', None, 'front'), as said below
- child_map: int32 [4, 8], replicated, may hold values from 0 to 31, as said below
Outputs:
- factored: float32 [8, 4, 128, 4, 8, 128], P(None, 'leaf', None, None, 'front')
Inputs may be any that keep to these rules, and one draw needn't show every extreme that they name: The blocks of one subtree go to distinct parent blocks, and child_map[c, j] modulo 8 equals j. front_entries is symmetric and positive definite, with its diagonal in 6 to 9. `child_blocks`: each subtree's block is symmetric with diagonal in 6 to 9 and small independent entries elsewhere.
All inputs are finite; a program needn't handle non-finite values.
Results may differ from a plain program's by a relative error of at most 0.0012.
Values may be sent and summed in bfloat16 or wider, within the bound.
A program may use at most 128 MiB of HBM per device.

v0:
```python
import jax
import jax.numpy as jnp
from jax import lax
from jax.sharding import PartitionSpec as P

KS = 8


def broadcast(x, axis, root):
    mine = lax.axis_index(axis) == root
    return lax.psum(jnp.where(mine, x, jnp.zeros_like(x)), axis)


def for_sending(x):
    return jax.tree.map(lambda a: a.astype(jnp.bfloat16) if a.dtype == jnp.float32 else a, x)


def on_device(front_entries, child_panels, child_blocks, child_map):
    leaf_count = lax.axis_size("leaf")
    front_count = lax.axis_size("front")
    leaf_id = lax.axis_index("leaf")
    front_id = lax.axis_index("front")
    row_blocks = front_entries.shape[0]
    block_size = front_entries.shape[2]
    col_blocks = front_entries.shape[3]
    spread = front_count // leaf_count
    own_rows = child_panels[0]
    own_block = child_blocks[0]
    given = own_block.astype(jnp.float32)
    product = lax.dot_general(
        lax.all_gather(child_panels[0], "front", axis=0, tiled=True),
        own_rows,
        (((1,), (1,)), ((), ())),
        preferred_element_type=jnp.float32,
    )
    update = (given - product).astype(jnp.bfloat16)
    row_targets = lax.dynamic_index_in_dim(
        child_map.reshape(leaf_count, spread, leaf_count), leaf_id, 2, keepdims=False
    )
    col_targets = lax.dynamic_index_in_dim(child_map, front_id, 1, keepdims=False)
    row_onehot = (
        row_targets[:, :, None] // leaf_count == jnp.arange(row_blocks)[None, None, :]
    ).astype(jnp.float32)
    col_onehot = (col_targets[:, None] // front_count == jnp.arange(col_blocks)[None, :]).astype(
        jnp.float32
    )
    every = lax.all_gather(update[None], "leaf", axis=0, tiled=True)
    received = lax.dynamic_index_in_dim(
        every.reshape(leaf_count, spread, leaf_count, block_size, block_size),
        leaf_id,
        2,
        keepdims=False,
    )
    added = jnp.einsum(
        "cqr,cqxy,cs->rxsy",
        row_onehot,
        received.astype(jnp.float32),
        col_onehot,
        precision=lax.Precision.HIGHEST,
    )
    assembled = front_entries.reshape(
        row_blocks * block_size, col_blocks * block_size
    ) + added.reshape(row_blocks * block_size, col_blocks * block_size)
    global_rows = jnp.arange(row_blocks) * leaf_count + leaf_id
    global_cols = jnp.arange(col_blocks) * front_count + front_id
    columns = []
    for pivot_index in range(KS):
        col_local = pivot_index // front_count
        col_owner = pivot_index % front_count
        column = assembled[:, col_local * block_size : (col_local + 1) * block_size]
        columns.append(
            broadcast(column.astype(jnp.bfloat16), "front", col_owner).astype(column.dtype)
        )
    separator = jnp.concatenate(columns, axis=1)
    width = KS * block_size
    top_blocks = -(-KS // leaf_count)
    diagonal_rows = lax.all_gather(
        separator[: top_blocks * block_size].astype(jnp.bfloat16), "leaf", axis=0, tiled=True
    ).astype(jnp.float32)
    diagonal_rows = jnp.swapaxes(
        diagonal_rows.reshape(leaf_count, top_blocks, block_size, width), 0, 1
    )
    diagonal_rows = diagonal_rows.reshape(top_blocks * leaf_count * block_size, width)
    factor = jnp.linalg.cholesky(diagonal_rows)
    solved = lax.linalg.triangular_solve(
        factor, separator, left_side=False, lower=True, transpose_a=True
    )
    row_global = (global_rows[:, None] * block_size + jnp.arange(block_size)[None, :]).reshape(-1)
    solved = jnp.where(row_global[:, None] >= jnp.arange(width)[None, :], solved, 0.0)
    chosen = lax.dynamic_index_in_dim(
        solved.reshape(col_blocks, spread, block_size, width),
        front_id // leaf_count,
        1,
        keepdims=False,
    )
    matching = broadcast(for_sending(chosen), "leaf", front_id % leaf_count).astype(chosen.dtype)
    assembled = assembled - lax.dot_general(
        solved,
        matching.reshape(col_blocks * block_size, width),
        (((1,), (1,)), ((), ())),
        precision=lax.Precision.HIGHEST,
        preferred_element_type=jnp.float32,
    )
    col_local = 0
    col_global = col_local * front_count + front_id
    offset = jnp.minimum(col_global, KS - 1) * block_size
    picked = lax.dynamic_slice_in_dim(solved, offset, block_size, 1)
    current = assembled[:, col_local * block_size : (col_local + 1) * block_size]
    assembled = assembled.at[:, col_local * block_size : (col_local + 1) * block_size].set(
        jnp.where(col_global < KS, picked, current)
    )
    shaped = assembled.reshape(row_blocks, block_size, col_blocks, block_size)
    keep_rows = global_rows[:, None] >= KS
    keep_cols = global_cols[None, :] < KS
    keeping = jnp.logical_or(keep_rows, keep_cols)
    result = jnp.where(keeping[:, None, :, None], shaped, 0.0)
    return result.reshape(row_blocks, 1, block_size, col_blocks, 1, block_size)


def solution(mesh):
    placed = (
        P(None, "leaf", None, None, "front", None),
        P("leaf", "front", None),
        P("leaf", None, "front"),
        P(),
    )
    return jax.shard_map(
        on_device,
        mesh=mesh,
        in_specs=placed,
        out_specs=P(None, "leaf", None, None, "front", None),
        check_vma=False,
    )
```

profile of v0, /device:TPU:0, one launch (start us, length us, event | category | flops | bytes accessed | tf_op | source)
XLA Modules:
  0.0 632.6 jit_solution(15528287623044052167)
XLA Ops:
  7.3 45.1 %all-gather.8.cloned.1.call-done = bf16[1,1024,512]{2,1,0:T(8,128)(2,1)} async-done(((bf16[1,128,512]{2,1,0:T(8,128)(2,1)}), bf16[1,1024,512]{2,1,0:T(8,128)(2,1)}) %all-gather.8.cloned.1.call-update) | async-done | bytes 1048592 | tf_op jit(solution)/shard_map/all_gather | solution.py:31
  56.9 13.7 %all-gather.10.cloned.1.call-done = bf16[4096,128]{1,0:T(8,128)(2,1)} async-done(((bf16[1024,128]{1,0:T(8,128)(2,1)}), bf16[4096,128]{1,0:T(8,128)(2,1)}) %all-gather.10.cloned.1.call-update) | async-done | bytes 1048592 | tf_op jit(solution)/shard_map/all_gather | solution.py:47
  79.7 105.6 %all-reduce.7.cloned.1.call-done = (bf16[1024,128]{1,0:T(8,128)(2,1)}, bf16[1024,128]{1,0:T(8,128)(2,1)}, bf16[1024,128]{1,0:T(8,128)(2,1)}, bf16[1024,128]{1,0:...) async-done(((bf16[1024,128]{1,0:T(8,128)(2,1)}, bf16[1024,128]{1,0:T(8,128)(2,1)}, ...) | async-done | bytes 2097168 | tf_op jit(solution)/shard_map/psum | solution.py:11
  193.8 21.3 %all-gather.6.cloned.1.call-done = bf16[1024,1024]{1,0:T(8,128)(2,1)} async-done(((bf16[256,1024]{1,0:T(8,128)(2,1)}), bf16[1024,1024]{1,0:T(8,128)(2,1)}) %all-gather.6.cloned.1.call-update) | async-done | bytes 2097168 | tf_op jit(solution)/shard_map/all_gather | solution.py:77
  215.2 4.6 copy.8
  219.7 5.5 reshape.251
  225.2 5.8 copy.9
  231.0 4.4 fusion
  237.4 11.7 %cholesky.224 = f32[128,128]{1,0:T(8,128)S(1)} custom-call(f32[128,128]{1,0:T(8,128)S(1)} %cholesky.583), custom_call_target="Cholesky" | custom-call | tf_op jit(solution)/shard_map/jit(cholesky)/cholesky | solution.py:84
  251.6 9.8 %custom-call.62 = f32[1,128,128]{1,2,0:T(8,128)S(1)} custom-call(f32[1,128,128]{2,1,0:T(8,128)S(1)} %get-tuple-element.98), custom_call_target="InvertDiagBlocksLowerTriangular" | custom-call | tf_op jit(solution)/shard_map/jit(cholesky)/cholesky | solution.py:84
  265.4 11.9 %cholesky.245 = f32[128,128]{1,0:T(8,128)S(1)} custom-call(f32[128,128]{1,0:T(8,128)S(1)} %cholesky.587), custom_call_target="Cholesky" | custom-call | tf_op jit(solution)/shard_map/jit(cholesky)/cholesky | solution.py:84
  277.9 9.8 %custom-call.63 = f32[1,128,128]{1,2,0:T(8,128)S(1)} custom-call(f32[1,128,128]{2,1,0:T(8,128)S(1)} %get-tuple-element.95), custom_call_target="InvertDiagBlocksLowerTriangular" | custom-call | tf_op jit(solution)/shard_map/jit(cholesky)/cholesky | solution.py:84
  291.0 11.7 %cholesky.470 = f32[128,128]{1,0:T(8,128)S(1)} custom-call(f32[128,128]{1,0:T(8,128)S(1)} %cholesky.592), custom_call_target="Cholesky" | custom-call | tf_op jit(solution)/shard_map/jit(cholesky)/cholesky | solution.py:84
  303.4 9.8 %custom-call.64 = f32[1,128,128]{1,2,0:T(8,128)S(1)} custom-call(f32[1,128,128]{2,1,0:T(8,128)S(1)} %get-tuple-element.92), custom_call_target="InvertDiagBlocksLowerTriangular" | custom-call | tf_op jit(solution)/shard_map/jit(cholesky)/cholesky | solution.py:84
  316.7 11.9 %cholesky.489 = f32[128,128]{1,0:T(8,128)S(1)} custom-call(f32[128,128]{1,0:T(8,128)S(1)} %cholesky.597), custom_call_target="Cholesky" | custom-call | tf_op jit(solution)/shard_map/jit(cholesky)/cholesky | solution.py:84
  329.3 9.8 %custom-call.65 = f32[1,128,128]{1,2,0:T(8,128)S(1)} custom-call(f32[1,128,128]{2,1,0:T(8,128)S(1)} %get-tuple-element.89), custom_call_target="InvertDiagBlocksLowerTriangular" | custom-call | tf_op jit(solution)/shard_map/jit(cholesky)/cholesky | solution.py:84
  342.5 11.7 %cholesky.508 = f32[128,128]{1,0:T(8,128)S(1)} custom-call(f32[128,128]{1,0:T(8,128)S(1)} %cholesky.602), custom_call_target="Cholesky" | custom-call | tf_op jit(solution)/shard_map/jit(cholesky)/cholesky | solution.py:84
  354.9 10.2 %custom-call.66 = f32[1,128,128]{1,2,0:T(8,128)S(1)} custom-call(f32[1,128,128]{2,1,0:T(8,128)S(1)} %get-tuple-element.86), custom_call_target="InvertDiagBlocksLowerTriangular" | custom-call | tf_op jit(solution)/shard_map/jit(cholesky)/cholesky | solution.py:84
  368.4 11.7 %cholesky.528 = f32[128,128]{1,0:T(8,128)S(1)} custom-call(f32[128,128]{1,0:T(8,128)S(1)} %cholesky.607), custom_call_target="Cholesky" | custom-call | tf_op jit(solution)/shard_map/jit(cholesky)/cholesky | solution.py:84
  380.8 9.8 %custom-call.67 = f32[1,128,128]{1,2,0:T(8,128)S(1)} custom-call(f32[1,128,128]{2,1,0:T(8,128)S(1)} %get-tuple-element.83), custom_call_target="InvertDiagBlocksLowerTriangular" | custom-call | tf_op jit(solution)/shard_map/jit(cholesky)/cholesky | solution.py:84
  393.6 11.7 %cholesky.548 = f32[128,128]{1,0:T(8,128)S(1)} custom-call(f32[128,128]{1,0:T(8,128)S(1)} %cholesky.612), custom_call_target="Cholesky" | custom-call | tf_op jit(solution)/shard_map/jit(cholesky)/cholesky | solution.py:84
  405.9 9.8 %custom-call.68 = f32[1,128,128]{1,2,0:T(8,128)S(1)} custom-call(f32[1,128,128]{2,1,0:T(8,128)S(1)} %get-tuple-element.80), custom_call_target="InvertDiagBlocksLowerTriangular" | custom-call | tf_op jit(solution)/shard_map/jit(cholesky)/cholesky | solution.py:84
  418.3 11.7 %cholesky.566 = f32[128,128]{1,0:T(8,128)S(1)} custom-call(f32[128,128]{1,0:T(8,128)S(1)} %convolution_subtract_fusion.13), custom_call_target="Cholesky" | custom-call | tf_op jit(solution)/shard_map/jit(cholesky)/cholesky | solution.py:84
  440.4 4.8 select_select_fusion
  445.3 22.8 %while.2 = (s32[]{:T(128)}, f32[1024,1024]{1,0:T(8,128)}, s32[8,2]{0,1:T(2,128)S(1)}, f32[8,128,128]{2,1,0:T(8,128)S(1)}, s32[]{:T(128)}) while((s32[]{:T(128)}, f32[1024,1024]{1,0:T(8,128)}, s32[8,2]{0,1:T(2,128)S(1)}, f32[8,128,128]{2,1,0:T(8,128)S(1)}, s32[]{:T(128)}) %tuple.77), condition=%wide.while_cond.1, body=%wide.while_body.1.sunk | while | flops 2 | bytes 131189 | solution.py:85
  468.1 78.8 %custom-call.69 = f32[8,128,128]{1,2,0:T(8,128)S(1)} custom-call(f32[8,128,128]{2,1,0:T(8,128)S(1)} %get-tuple-element.24), custom_call_target="InvertDiagBlocksLowerTriangular" | custom-call | tf_op jit(solution)/shard_map/triangular_solve | solution.py:85
  562.5 3.9 convolution_subtract_fusion.3
  566.9 4.3 convolution_subtract_fusion.5
  575.0 4.5 fusion.1
  579.5 30.9 %all-reduce.5.cloned.1.call-done = bf16[512,1024]{1,0:T(8,128)(2,1)} async-done(((bf16[512,1024]{1,0:T(8,128)(2,1)}), bf16[512,1024]{1,0:T(8,128)(2,1)}) %all-reduce.5.cloned.1.call-update) | async-done | bytes 1048592 | tf_op jit(solution)/shard_map/psum | solution.py:11
  610.4 6.6 %convolution_subtract_fusion = f32[1024,512]{1,0:T(8,128)S(1)} fusion(f32[1024,512]{1,0:T(8,128)} %copy-done.1, f32[1024,1024]{1,0:T(8,128)} %fusion.1, bf16[512,1024]{1,0:T(8,128)(2,1)} %all-reduce.5.cloned.1.call-done), kind=kOutput, calls=%fused_computation.30 | convolution fusion | flops 6442975232 | bytes 9437184 | tf_op jit(solution)/shard_map/dot_general | solution.py:97
  620.6 5.0 broadcast_select_fusion
  (152 shorter events, 105.3 us)
Async XLA Ops:
  6.5 45.8 %all-gather.8.cloned.1.call-start = ((), (), s32[]{:S(2)}) async-start(), calls=%async_computation.2 | async-start | bytes 1179648 | tf_op jit(solution)/shard_map/all_gather | solution.py:31
  7.3 63.3 %all-gather.10.cloned.1.call-start = ((), (), s32[]{:S(2)}) async-start(), calls=%async_computation.3 | async-start | bytes 1310720 | tf_op jit(solution)/shard_map/all_gather | solution.py:47
  54.9 130.4 %all-reduce.7.cloned.1.call-start = ((), (), s32[]{:S(2)}) async-start(), calls=%async_computation.4 | async-start | bytes 4194304 | tf_op jit(solution)/shard_map/psum | solution.py:11
  72.1 3.7 copy-start.3
  76.3 1.3 copy-start.1
  79.6 135.5 %all-gather.6.cloned.1.call-start = ((), (), s32[]{:S(2)}) async-start(), calls=%async_computation | async-start | bytes 2621440 | tf_op jit(solution)/shard_map/all_gather | solution.py:77
  185.3 7.3 %copy-start.5 = (bf16[1024,128]{1,0:T(8,128)(2,1)S(1)}, bf16[1024,128]{1,0:T(8,128)(2,1)}, u32[]{:S(2)}) copy-start(bf16[1024,128]{1,0:T(8,128)(2,1)} %get-tuple-element.40) | copy-start | bytes 786436
  193.5 416.9 %all-reduce.5.cloned.1.call-start = ((), (), s32[]{:S(2)}) async-start(), calls=%async_computation.1 | async-start | bytes 2097152 | tf_op jit(solution)/shard_map/psum | solution.py:11
  235.4 1.9 copy-start
  440.4 106.5 %copy-start.9 = (bf16[1024,128]{1,0:T(8,128)(2,1)S(1)}, bf16[1024,128]{1,0:T(8,128)(2,1)}, u32[]{:S(2)}) copy-start(bf16[1024,128]{1,0:T(8,128)(2,1)} %get-tuple-element.33) | copy-start | bytes 786436
  445.3 102.1 %copy-start.10 = (bf16[1024,128]{1,0:T(8,128)(2,1)S(1)}, bf16[1024,128]{1,0:T(8,128)(2,1)}, u32[]{:S(2)}) copy-start(bf16[1024,128]{1,0:T(8,128)(2,1)} %get-tuple-element.34) | copy-start | bytes 786436
  546.9 2.5 copy-start.8
  548.8 3.2 copy-start.7
  551.9 3.1 copy-start.11
  555.0 3.4 copy-start.4
  558.4 4.0 copy-start.6
  571.9 2.3 copy-start.2
Sparse Core Ops, SparseCore 0:
  9.5 42.8 all-gather.7
  55.0 15.5 all-gather.9
  79.8 105.4 all-reduce.6
  193.7 21.4 all-gather.5
  574.3 36.0 all-reduce.4
where the time goes:
time: 640 us; the launch traced here: 633 us
  other arithmetic  278 us (43%)
  waiting for transfers between devices  217 us (34%)
  matrix products  60.6 us (9%)
  local copies, waits for them, and re-layouts  57.3 us (9%)
  between operations  19.3 us (3%)
    another operation x30, other arithmetic, on_device(): factor = jnp.linalg.cholesky(diagonal_rows)  172 us
    psum x2, waiting for transfers between devices, broadcast(): return lax.psum(jnp.where(mine, x, jnp.zeros_like(x)), axis)  137 us
    another operation x3, other arithmetic, on_device(): lax.linalg.triangular_solve(factor, separator, left_side=False, lower=Tru...  83.6 us
    all_gather x1, waiting for transfers between devices, on_device(): lax.all_gather(child_panels[0], 'front', axis=0, tiled=True)  45.1 us
    another operation x15, matrix products, on_device(): lax.linalg.triangular_solve(factor, separator, left_side=False, lower=Tru...  24.7 us
    another operation x14, matrix products, on_device(): factor = jnp.linalg.cholesky(diagonal_rows)  23.1 us
    another operation x24, local copies, waits for them, and re-layouts  22.7 us
    all_gather x1, waiting for transfers between devices, on_device(): lax.all_gather(separator[:top_blocks * block_size].astype(jnp.bfloat16),...  21.3 us
  transfers between devices with their start and end apart: 5, of which 5 were waited for; matrix products, arithmetic and copies ran while one was open for 1% of the time, Pallas kernels for 0%

commit v1 on v0

v1 whole, which is shorter than its diff:
```python
import functools

import jax
import jax.numpy as jnp
from jax import lax
from jax.experimental import pallas as pl
from jax.experimental.pallas import tpu as pltpu
from jax.sharding import PartitionSpec as P

KS = 8
NT = (((1,), (1,)), ((), ()))
NN = (((1,), (0,)), ((), ()))
VMEM = pl.BlockSpec(memory_space=pltpu.VMEM)
SMEM = pl.BlockSpec(memory_space=pltpu.SMEM)
LIMIT = 56 * 1024 * 1024


def dot(a, b, dims):
    return lax.dot_general(a, b, dims, preferred_element_type=jnp.float32)


def halves(x):
    high = x.astype(jnp.bfloat16)
    return high, (x - high.astype(jnp.float32)).astype(jnp.bfloat16)


def dot3(a, b, dims):
    return dot(a[0], b[0], dims) + (dot(a[0], b[1], dims) + dot(a[1], b[0], dims))


def factor_block(a_ref, u_ref, z_ref):
    size = a_ref.shape[0]
    tiles = size // 8
    sub = lax.broadcasted_iota(jnp.int32, (8, size), 0)
    lane = lax.broadcasted_iota(jnp.int32, (8, size), 1)
    a = [a_ref[8 * t : 8 * t + 8, :] for t in range(tiles)]
    z = [jnp.where(lane == sub + 8 * t, 1.0, 0.0).astype(jnp.float32) for t in range(tiles)]

    def row(tile, s):
        return jnp.broadcast_to(tile[s : s + 1, :], (8, size))

    def column(tile, j):
        return jnp.broadcast_to(tile[:, j : j + 1], (8, size))

    for j in range(0, size, 2):
        t0, s = j // 8, j % 8
        r0, r1 = row(a[t0], s), row(a[t0], s + 1)
        q0, q1 = row(z[t0], s), row(z[t0], s + 1)
        p00, p01, p11 = column(r0, j), column(r0, j + 1), column(r1, j + 1)
        det = p00 * p11 - p01 * p01
        inv = pl.reciprocal(det, approx=True)
        inv = inv * (2.0 - det * inv)
        e0, e1 = (p11 * r0 - p01 * r1) * inv, (p00 * r1 - p01 * r0) * inv
        g0, g1 = (p11 * q0 - p01 * q1) * inv, (p00 * q1 - p01 * q0) * inv
        for t in range(t0, tiles):
            if t == t0 and s == 6:
                continue
            x, y = column(a[t], j), column(a[t], j + 1)
            if t == t0:
                x, y = jnp.where(sub > s + 1, x, 0.0), jnp.where(sub > s + 1, y, 0.0)
            a[t] = a[t] - (x * e0 + y * e1)
            z[t] = z[t] - (x * g0 + y * g1)
        d0 = lax.rsqrt(p00)
        ratio = p01 * d0 * d0
        d1 = lax.rsqrt(p11 - ratio * p01)
        u_ref[j : j + 1, :] = (r0 * d0)[:1]
        u_ref[j + 1 : j + 2, :] = ((r1 - ratio * r0) * d1)[:1]
        z_ref[j : j + 1, :] = (q0 * d0)[:1]
        z_ref[j + 1 : j + 2, :] = ((q1 - ratio * q0) * d1)[:1]


def cholesky_kernel(place, blocks_ref, l_ref, z_ref, a_ref, d_ref, u_ref):
    size = blocks_ref.shape[1]
    for j in range(KS):
        for i in range(j, KS):
            at = place(i, j)
            a_ref[i * size : (i + 1) * size, j * size : (j + 1) * size] = blocks_ref[
                at * size : (at + 1) * size, :
            ].astype(jnp.float32)
            if i > j:
                l_ref[j * size : (j + 1) * size, i * size : (i + 1) * size] = jnp.zeros(
                    (size, size), jnp.float32
                )
    d_ref[...] = a_ref[:size, :size]
    keep = lax.broadcasted_iota(jnp.int32, (size, size), 0) >= lax.broadcasted_iota(
        jnp.int32, (size, size), 1
    )

    def step(k, carry):
        z_now = z_ref.at[pl.ds(pl.multiple_of(k * size, size), size), :]
        factor_block(d_ref, u_ref, z_now)
        for now in range(KS):

            @pl.when(k == now)
            def _():
                low, high = now * size, (now + 1) * size
                l_ref[low:high, low:high] = jnp.where(keep, u_ref[...].T, 0.0)
                if now + 1 == KS:
                    return
                panel = dot3(halves(a_ref[high:, low:high]), halves(z_now[...]), NT)
                l_ref[high:, low:high] = panel
                parts = halves(panel)
                for j in range(now + 1, KS):
                    skip = (j - now - 1) * size
                    left = tuple(x[skip:] for x in parts)
                    right = tuple(x[skip : skip + size] for x in parts)
                    at = j * size
                    fresh = a_ref[at:, at : at + size] - dot3(left, right, NT)
                    if j == now + 1:
                        d_ref[...] = fresh[:size]
                    a_ref[at:, at : at + size] = fresh

        return carry

    lax.fori_loop(0, KS, step, 0)


def assemble_kernel(leaf_count, front_count, where_ref, map_ref, got_ref, front_ref, out_ref):
    children, spread, size, _ = got_ref.shape
    leaf_id, front_id = where_ref[0], where_ref[1]
    rows = out_ref.shape[1]
    for s in range(out_ref.shape[0]):
        out_ref[s] = front_ref[pl.ds(s, rows, stride=out_ref.shape[0]), :]
    for c in range(children):
        col = map_ref[c, front_id] // front_count
        for q in range(spread):
            at = pl.multiple_of(map_ref[c, leaf_id + leaf_count * q] // leaf_count * size, size)
            out_ref[col, pl.ds(at, size), :] += got_ref[c, q].astype(jnp.float32)


def solve_kernel(
    leaf_count, first, where_ref, l_ref, z_ref, rows_ref, tops_ref, full_ref, out_ref, s_ref, w_ref
):
    col_blocks, all_rows, size = full_ref.shape
    top = tops_ref.shape[0] // leaf_count // size
    rows = all_rows - top * size
    leaf_id, front_id = where_ref[0], where_ref[1]
    low = jnp.bfloat16
    for k in range(KS):
        at = slice(k * size, (k + 1) * size)
        inverse = z_ref[at, :].astype(low)
        own = rows_ref[k * rows : (k + 1) * rows, :]
        source = ((k % leaf_count) * top + k // leaf_count) * size
        met = tops_ref[source : source + size, first * size :]
        if k:
            before = l_ref[at, : k * size].astype(low)
            own = (own.astype(jnp.float32) - dot(s_ref[:, : k * size], before, NT)).astype(low)
            met = (met.astype(jnp.float32) - dot(before, w_ref[: k * size, :], NN)).astype(low)
        solved = dot(own, inverse, NT)
        s_ref[:, at] = solved.astype(low)
        w_ref[at, :] = dot(inverse, met, NN).astype(low)

        @pl.when(front_id == k)
        def _():
            out_ref[pl.ds(top * size * col_blocks, rows, stride=col_blocks), :] = solved
            for t in range(top):
                from_row = pl.multiple_of((t * leaf_count + leaf_id) * size, size)
                out_ref[pl.ds(t * size * col_blocks, size, stride=col_blocks), :] = l_ref[
                    pl.ds(from_row, size), at
                ]

    def complement(s):
        chunk = 256 if rows % 256 == 0 else size
        for r in range(0, rows, chunk):
            left = s_ref[r : r + chunk, :]
            right = w_ref[:, (s - first) * size : (s - first + 1) * size]
            begin = top * size + r
            out_ref[pl.ds(begin * col_blocks + s, chunk, stride=col_blocks), :] = full_ref[
                s, begin : begin + chunk, :
            ] - dot(left, right, NN)
        out_ref[pl.ds(s, top * size, stride=col_blocks), :] = jnp.zeros(
            (top * size, size), jnp.float32
        )

    for s in range(first, col_blocks):
        if s == 0:
            pl.when(front_id >= KS)(functools.partial(complement, s))
        else:
            complement(s)


def on_device(front_entries, child_panels, child_blocks, child_map):
    leaf_count = lax.axis_size("leaf")
    front_count = lax.axis_size("front")
    place = jnp.stack([lax.axis_index("leaf"), lax.axis_index("front")]).astype(jnp.int32)
    row_blocks, _, size, col_blocks, _, _ = front_entries.shape
    children = child_map.shape[0]
    spread = child_map.shape[1] // leaf_count
    rows = row_blocks * size
    top = KS // leaf_count
    first = KS // front_count
    params = pltpu.CompilerParams(vmem_limit_bytes=LIMIT)
    product = lax.dot_general(
        lax.all_gather(child_panels[0], "front", axis=0, tiled=True),
        child_panels[0],
        NT,
        preferred_element_type=jnp.float32,
    )
    update = (child_blocks[0].astype(jnp.float32) - product).astype(jnp.bfloat16)
    got = lax.all_to_all(
        update.reshape(spread, leaf_count, size, size), "leaf", split_axis=1, concat_axis=0
    )
    full = pl.pallas_call(
        functools.partial(assemble_kernel, leaf_count, front_count),
        out_shape=jax.ShapeDtypeStruct((col_blocks, rows, size), jnp.float32),
        in_specs=[SMEM, SMEM, VMEM, VMEM],
        out_specs=VMEM,
        compiler_params=params,
    )(
        place,
        child_map,
        got.reshape(children, spread, size, size),
        front_entries.reshape(rows * col_blocks, size),
    )
    tops = full[:, : top * size].astype(jnp.bfloat16)
    corner = lax.all_gather(tops[0], ("leaf", "front"), axis=0, tiled=True)
    below = lax.all_gather(full[0, top * size :].astype(jnp.bfloat16), "front", axis=0, tiled=True)
    across = jnp.swapaxes(tops, 0, 1).reshape(top * size, col_blocks * size)
    across = lax.all_gather(across, "leaf", axis=0, tiled=True)
    width = KS * size

    def corner_place(i, j):
        return ((i % leaf_count) * front_count + j) * top + i // leaf_count

    lower, inverses = pl.pallas_call(
        functools.partial(cholesky_kernel, corner_place),
        out_shape=[
            jax.ShapeDtypeStruct((width, width), jnp.float32),
            jax.ShapeDtypeStruct((width, size), jnp.float32),
        ],
        in_specs=[VMEM],
        out_specs=[VMEM, VMEM],
        scratch_shapes=[
            pltpu.VMEM((width, width), jnp.float32),
            pltpu.VMEM((size, size), jnp.float32),
            pltpu.VMEM((size, size), jnp.float32),
        ],
        compiler_params=params,
        cost_estimate=pl.CostEstimate(
            flops=8 * width**3, bytes_accessed=8 * width * width, transcendentals=0
        ),
    )(corner)
    result = pl.pallas_call(
        functools.partial(solve_kernel, leaf_count, first),
        out_shape=jax.ShapeDtypeStruct((rows * col_blocks, size), jnp.float32),
        in_specs=[SMEM] + [VMEM] * 5,
        out_specs=VMEM,
        scratch_shapes=[
            pltpu.VMEM((rows - top * size, width), jnp.bfloat16),
            pltpu.VMEM((width, (col_blocks - first) * size), jnp.bfloat16),
        ],
        compiler_params=params,
    )(place, lower, inverses, below, across, full)
    return result.reshape(row_blocks, 1, size, col_blocks, 1, size)


def solution(mesh):
    placed = (
        P(None, "leaf", None, None, "front", None),
        P("leaf", "front", None),
        P("leaf", None, "front"),
        P(),
    )
    return jax.shard_map(
        on_device,
        mesh=mesh,
        in_specs=placed,
        out_specs=P(None, "leaf", None, None, "front", None),
        check_vma=False,
    )
```

time: 640 us -> 229 us (0.36); the launches traced: 633 us -> 229 us
  other arithmetic: 278 us -> 2.29 us
  waiting for transfers between devices: 217 us -> 104 us
  Pallas kernels: 0 us -> 100 us
  matrix products: 60.6 us -> 1.76 us
  local copies, waits for them, and re-layouts: 57.3 us -> 3.46 us
    another operation x34 -> x2, other arithmetic: 257 us -> 2.29 us  [the longest x30 172 us: on_device(): factor = jnp.linalg.cholesky(diagonal_rows)]
    psum x2 -> x0, waiting for transfers between devices: 137 us -> none  [broadcast(): return lax.psum(jnp.where(mine, x, jnp.zeros_like(x)), axis)]
    pallas_call x0 -> x3, Pallas kernels: none -> 100 us  [the longest x1 85.6 us: on_device(): pl.pallas_call(functools.partial(cholesky_kernel, corner_place), out_shap...]
    another operation x29 -> x0, matrix products: 47.7 us -> none  [the longest x15 24.7 us: on_device(): lax.linalg.triangular_solve(factor, separator, left_side=False, lower=Tru...]
    another operation x34 -> x1, local copies, waits for them, and re-layouts: 25.3 us -> 0.72 us  [on_device(): lax.all_to_all(update.reshape(spread, leaf_count, size, size), 'leaf', sp...]
    all_gather x2 -> x3, waiting for transfers between devices: 35.1 us -> 52.9 us  [the longest x1 52.9 us: on_device(): corner = lax.all_gather(tops[0], ('leaf', 'front'), axis=0, tiled=True)]
    reshape x5 -> x1, local copies, waits for them, and re-layouts: 18.3 us -> 0.73 us  [on_device(): across = jnp.swapaxes(tops, 0, 1).reshape(top * size, col_blocks * size)]
    select_n x7 -> x0, other arithmetic: 14 us -> none  [the longest x1 4.98 us: on_device(): result = jnp.where(keeping[:, None, :, None], shaped, 0.0)]
  transfers between devices with their start and end apart: 5 -> 5, of which waited for: 5 -> 3; matrix products, arithmetic and copies ran while one was open for 1% -> 1% of each run, Pallas kernels for 0% -> 37%
where the time goes in v1:
time: 229 us
  waiting for transfers between devices  104 us (45%)
  Pallas kernels  100 us (44%)
  between operations  13.2 us (6%)
  starting transfers between devices  3.54 us (2%)
  local copies, waits for them, and re-layouts  3.46 us (2%)
  other arithmetic  2.29 us (1%)
    pallas_call x1, Pallas kernels, on_device(): pl.pallas_call(functools.partial(cholesky_kernel, corner_place), out_shap...  85.6 us
    all_gather x1, waiting for transfers between devices, on_device(): corner = lax.all_gather(tops[0], ('leaf', 'front'), axis=0, tiled=True)  52.9 us
    all_gather x1, waiting for transfers between devices, on_device(): lax.all_gather(child_panels[0], 'front', axis=0, tiled=True)  45.1 us
    pallas_call x1, Pallas kernels, on_device(): pl.pallas_call(functools.partial(solve_kernel, leaf_count, first), out_sh...  11.5 us
    all_to_all x1, waiting for transfers between devices, on_device(): lax.all_to_all(update.reshape(spread, leaf_count, size, size), 'leaf', sp...  5.39 us
  transfers between devices with their start and end apart: 5, of which 3 were waited for; matrix products, arithmetic and copies ran while one was open for 1% of the time, Pallas kernels for 37%

profile of v1, /device:TPU:0, one launch (start us, length us, event | category | flops | bytes accessed | tf_op | source)
XLA Modules:
  0.0 228.8 jit_solution(9767071741284171613)
XLA Ops:
  6.5 0.0 all-gather.10.cloned.1.call-start
  6.5 0.7 all-gather.10.cloned.1.call-update
  7.3 45.1 %all-gather.10.cloned.1.call-done = bf16[1,1024,512]{2,1,0:T(8,128)(2,1)} async-done(((bf16[1,128,512]{2,1,0:T(8,128)(2,1)}), bf16[1,1024,512]{2,1,0:T(8,128)(2,1)}) %all-gather.10.cloned.1.call-update) | async-done | bytes 1048592 | tf_op jit(solution)/shard_map/all_gather | solution.py:194
  52.4 1.8 fusion
  54.1 0.7 copy.10
  54.9 3.4 %all-to-all-start = ((bf16[1,2,4,128,128]{4,3,1,0,2:T(8,128)(2,1)}), bf16[1,2,4,128,128]{4,3,1,0,2:T(8,128)(2,1)S(1)}, u32[]{:S(2)}, u32[]{:S(2)}) async-start(bf16[1,2,4,128,128]{4,3,1,0,2:T(8,128)(2,1)} %copy.10), calls=%async_computation | async-start | bytes 524288 | tf_op jit(solution)/shard_map/all_to_all | solution.py:200
  58.3 0.0 all-gather.12.cloned.1.call-start
  58.3 0.6 pad_add_fusion.where_ref
  58.9 5.4 %all-to-all-done = bf16[1,2,4,128,128]{4,3,1,0,2:T(8,128)(2,1)S(1)} async-done(((bf16[1,2,4,128,128]{4,3,1,0,2:T(8,128)(2,1)}), bf16[1,2,4,128,128]{4,3,1,0,2:T(8,128)(2,1)S(1)}, u32[]{:S(2)}, u32[]{:S(2)}) %all-to-all-start) | async-done | bytes 262176 | tf_op jit(solution)/shard_map/all_to_all | solution.py:200
  64.3 0.0 copy-start
  64.3 0.7 copy-done
  65.0 3.3 %shard_map.46.full_ref = f32[4,1024,128]{2,1,0:T(8,128)} custom-call(s32[2]{0:T(128)} %pad_add_fusion.where_ref, s32[4,8]{1,0:T(4,128)} %map_ref.1, bf16[4,2,128,128]{3,2,1,0:T(8,128)(2,1)} %bitcast.31, f32[4096,128]{1,0:T(8,128)} %bitcast.29), custom_call_target="tpu_custom_call" | custom-call | tf_op jit(solution)/shard_map/pallas_call | solution.py:203
  68.3 1.7 convert.5
  70.0 0.6 slice.15
  70.6 0.0 all-gather.12.cloned.1.call-update
  70.6 0.0 all-gather.8.cloned.1.call-start
  70.7 0.7 copy_bitcast_fusion
  71.4 0.0 all-gather.8.cloned.1.call-update
  71.4 0.0 all-gather.14.cloned.1.call-start
  71.5 0.7 slice.16
  72.2 0.0 all-gather.14.cloned.1.call-update
  72.2 52.9 %all-gather.12.cloned.1.call-done = bf16[1,8192,128]{2,1,0:T(8,128)(2,1)} async-done(((bf16[1,256,128]{2,1,0:T(8,128)(2,1)}), bf16[1,8192,128]{2,1,0:T(8,128)(2,1)}) %all-gather.12.cloned.1.call-update) | async-done | bytes 2097168 | tf_op jit(solution)/shard_map/all_gather | solution.py:216
  125.1 85.6 %shard_map.47 = (f32[1024,1024]{1,0:T(8,128)}, f32[1024,128]{1,0:T(8,128)}) custom-call(bf16[8192,128]{1,0:T(8,128)(2,1)} %bitcast.33), custom_call_target="tpu_custom_call" | custom-call | flops 8589934592 | bytes 8388608 | tf_op jit(solution)/shard_map/pallas_call | solution.py:225
  210.7 0.0 all-gather.8.cloned.1.call-done.tops_ref
  210.7 0.0 all-gather.14.cloned.1.call-done
  210.7 11.5 %shard_map.48 = f32[4096,128]{1,0:T(8,128)} custom-call(s32[2]{0:T(128)} %pad_add_fusion.where_ref, f32[1024,1024]{1,0:T(8,128)} %get-tuple-element.7.l_ref, f32[1024,128]{1,0:T(8,128)} %get-tuple-element.8.z_ref, bf16[6144,128]{1,0:T(8,128)(2,1)} %bitcast.30, bf16[1024,512]{1,0:T(8,128)(2,1)} %all-gather.8.cloned.1.call-done.tops_ref, ...), custom_call_target="tpu_custom_call" | custom-call | tf_op jit(solution)/shard_map/pallas_call | solution.py:243
Async XLA Ops:
  6.5 45.8 %all-gather.10.cloned.1.call-start = ((), (), s32[]{:S(2)}) async-start(), calls=%async_computation.2 | async-start | bytes 1179648 | tf_op jit(solution)/shard_map/all_gather | solution.py:194
  54.9 9.4 %all-to-all-start = ((bf16[1,2,4,128,128]{4,3,1,0,2:T(8,128)(2,1)}), bf16[1,2,4,128,128]{4,3,1,0,2:T(8,128)(2,1)S(1)}, u32[]{:S(2)}, u32[]{:S(2)}) async-start(bf16[1,2,4,128,128]{4,3,1,0,2:T(8,128)(2,1)} %copy.10), calls=%async_computation | async-start | bytes 524288 | tf_op jit(solution)/shard_map/all_to_all | solution.py:200
  58.3 66.9 %all-gather.12.cloned.1.call-start = ((), (), s32[]{:S(2)}) async-start(), calls=%async_computation.3 | async-start | bytes 2162688 | tf_op jit(solution)/shard_map/all_gather | solution.py:216
  64.3 0.7 copy-start
  70.6 140.1 %all-gather.8.cloned.1.call-start = ((), (), s32[]{:S(2)}) async-start(), calls=%async_computation.1 | async-start | bytes 1310720 | tf_op jit(solution)/shard_map/all_gather | solution.py:219
  71.4 139.3 %all-gather.14.cloned.1.call-start = ((), (), s32[]{:S(2)}) async-start(), calls=%async_computation.4 | async-start | bytes 1769472 | tf_op jit(solution)/shard_map/all_gather | solution.py:217
Sparse Core Ops, SparseCore 0:
  9.5 42.8 all-gather.9
  70.7 54.3 all-gather.11
  126.7 15.6 all-gather.7
  144.4 44.3 all-gather.13

commit v2 on v1

--- a/solution.py
+++ b/solution.py
@@ -42,31 +42,61 @@
     def column(tile, j):
         return jnp.broadcast_to(tile[:, j : j + 1], (8, size))
 
-    for j in range(0, size, 2):
-        t0, s = j // 8, j % 8
-        r0, r1 = row(a[t0], s), row(a[t0], s + 1)
-        q0, q1 = row(z[t0], s), row(z[t0], s + 1)
-        p00, p01, p11 = column(r0, j), column(r0, j + 1), column(r1, j + 1)
-        det = p00 * p11 - p01 * p01
-        inv = pl.reciprocal(det, approx=True)
-        inv = inv * (2.0 - det * inv)
-        e0, e1 = (p11 * r0 - p01 * r1) * inv, (p00 * r1 - p01 * r0) * inv
-        g0, g1 = (p11 * q0 - p01 * q1) * inv, (p00 * q1 - p01 * q0) * inv
-        for t in range(t0, tiles):
-            if t == t0 and s == 6:
-                continue
-            x, y = column(a[t], j), column(a[t], j + 1)
-            if t == t0:
-                x, y = jnp.where(sub > s + 1, x, 0.0), jnp.where(sub > s + 1, y, 0.0)
-            a[t] = a[t] - (x * e0 + y * e1)
-            z[t] = z[t] - (x * g0 + y * g1)
-        d0 = lax.rsqrt(p00)
-        ratio = p01 * d0 * d0
-        d1 = lax.rsqrt(p11 - ratio * p01)
-        u_ref[j : j + 1, :] = (r0 * d0)[:1]
-        u_ref[j + 1 : j + 2, :] = ((r1 - ratio * r0) * d1)[:1]
-        z_ref[j : j + 1, :] = (q0 * d0)[:1]
-        z_ref[j + 1 : j + 2, :] = ((q1 - ratio * q0) * d1)[:1]
+    for t0 in range(tiles):
+        base = 8 * t0
+        spread = [column(a[t0], base + k) for k in range(8)]
+        e = {(m, k): row(spread[k], m) for k in range(8) for m in range(k + 1)}
+        r = [row(a[t0], m) for m in range(8)]
+        q = [row(z[t0], m) for m in range(8)]
+        x = {t: [column(a[t], base + k) for k in range(8)] for t in range(t0 + 1, tiles)}
+        w, v, solved = [None] * 8, [None] * 8, {}
+        for j in range(0, 8, 2):
+            p00, p01, p11 = e[j, j], e[j, j + 1], e[j + 1, j + 1]
+            det = p00 * p11 - p01 * p01
+            inv = pl.reciprocal(det, approx=True)
+            inv = inv * (2.0 - det * inv)
+            c00, c01, c11 = p00 * inv, p01 * inv, p11 * inv
+
+            def pivot(first, second):
+                return c11 * first - c01 * second, c00 * second - c01 * first
+
+            for m in range(j + 2, 8):
+                solved[j, m], solved[j + 1, m] = pivot(e[j, m], e[j + 1, m])
+            for m in range(j + 2, 8):
+                for k in range(m, 8):
+                    e[m, k] = e[m, k] - (e[j, m] * solved[j, k] + e[j + 1, m] * solved[j + 1, k])
+            w[j], w[j + 1] = pivot(r[j], r[j + 1])
+            v[j], v[j + 1] = pivot(q[j], q[j + 1])
+            for m in range(j + 2, 8):
+                r[m] = r[m] - (e[j, m] * w[j] + e[j + 1, m] * w[j + 1])
+                q[m] = q[m] - (e[j, m] * v[j] + e[j + 1, m] * v[j + 1])
+            d0 = lax.rsqrt(p00)
+            ratio = p01 * d0 * d0
+            d1 = lax.rsqrt(p11 - ratio * p01)
+            at = base + j
+            u_ref[at : at + 1, :] = (r[j] * d0)[:1]
+            u_ref[at + 1 : at + 2, :] = ((r[j + 1] - ratio * r[j]) * d1)[:1]
+            z_ref[at : at + 1, :] = (q[j] * d0)[:1]
+            z_ref[at + 1 : at + 2, :] = ((q[j + 1] - ratio * q[j]) * d1)[:1]
+        if t0 + 1 == tiles:
+            break
+        for j in (4, 2, 0):
+            for i in (j, j + 1):
+                for k in range(j + 2, 8):
+                    w[i] = w[i] - solved[i, k] * w[k]
+                    v[i] = v[i] - solved[i, k] * v[k]
+        for t in range(t0 + 1, tiles):
+            y = x[t]
+            terms = [y[k] * w[k] for k in range(8)]
+            a[t] = a[t] - (
+                ((terms[0] + terms[1]) + (terms[2] + terms[3]))
+                + ((terms[4] + terms[5]) + (terms[6] + terms[7]))
+            )
+            terms = [y[k] * v[k] for k in range(8)]
+            z[t] = z[t] - (
+                ((terms[0] + terms[1]) + (terms[2] + terms[3]))
+                + ((terms[4] + terms[5]) + (terms[6] + terms[7]))
+            )
 
 
 def cholesky_kernel(place, blocks_ref, l_ref, z_ref, a_ref, d_ref, u_ref):
@@ -129,7 +159,7 @@
 
 
 def solve_kernel(
-    leaf_count, first, where_ref, l_ref, z_ref, rows_ref, tops_ref, full_ref, out_ref, s_ref, w_ref
+    leaf_count, front_count, first, where_ref, l_ref, z_ref, rows_ref, tops_ref, full_ref, out_ref, s_ref, w_ref
 ):
     col_blocks, all_rows, size = full_ref.shape
     top = tops_ref.shape[0] // leaf_count // size
@@ -139,9 +169,11 @@
     for k in range(KS):
         at = slice(k * size, (k + 1) * size)
         inverse = z_ref[at, :].astype(low)
-        own = rows_ref[k * rows : (k + 1) * rows, :]
-        source = ((k % leaf_count) * top + k // leaf_count) * size
-        met = tops_ref[source : source + size, first * size :]
+        distance = lax.rem(front_id - k + front_count, front_count)
+        own = rows_ref[pl.ds(pl.multiple_of(distance * rows, size), rows), :]
+        distance = lax.rem(leaf_id - k % leaf_count + leaf_count, leaf_count)
+        source = (distance * top + k // leaf_count) * size
+        met = tops_ref[pl.ds(pl.multiple_of(source, size), size), first * size :]
         if k:
             before = l_ref[at, : k * size].astype(low)
             own = (own.astype(jnp.float32) - dot(s_ref[:, : k * size], before, NT)).astype(low)
@@ -177,6 +209,14 @@
             pl.when(front_id >= KS)(functools.partial(complement, s))
         else:
             complement(s)
+
+
+def gather_by_distance(x, axis):
+    count = lax.axis_size(axis)
+    pieces = [x]
+    for d in range(1, count):
+        pieces.append(lax.ppermute(x, axis, [(i, (i + d) % count) for i in range(count)]))
+    return jnp.concatenate(pieces, axis=0)
 
 
 def on_device(front_entries, child_panels, child_blocks, child_map):
@@ -214,9 +254,9 @@
     )
     tops = full[:, : top * size].astype(jnp.bfloat16)
     corner = lax.all_gather(tops[0], ("leaf", "front"), axis=0, tiled=True)
-    below = lax.all_gather(full[0, top * size :].astype(jnp.bfloat16), "front", axis=0, tiled=True)
+    below = gather_by_distance(full[0, top * size :].astype(jnp.bfloat16), "front")
     across = jnp.swapaxes(tops, 0, 1).reshape(top * size, col_blocks * size)
-    across = lax.all_gather(across, "leaf", axis=0, tiled=True)
+    across = gather_by_distance(across, "leaf")
     width = KS * size
 
     def corner_place(i, j):
@@ -241,7 +281,7 @@
         ),
     )(corner)
     result = pl.pallas_call(
-        functools.partial(solve_kernel, leaf_count, first),
+        functools.partial(solve_kernel, leaf_count, front_count, first),
         out_shape=jax.ShapeDtypeStruct((rows * col_blocks, size), jnp.float32),
         in_specs=[SMEM] + [VMEM] * 5,
         out_specs=VMEM,

time: 229 us -> 204 us (0.89)
  Pallas kernels: 100 us -> 62.9 us
  starting transfers between devices: 3.54 us -> 15.6 us
    all_gather x1, waiting for transfers between devices: 52.9 us -> 14.8 us  [on_device(): corner = lax.all_gather(tops[0], ('leaf', 'front'), axis=0, tiled=True)]
    ppermute x0 -> x10, waiting for transfers between devices: none -> 37.8 us  [gather_by_distance(): lax.ppermute(x, axis, [(i, (i + d) % count) for i in range(count)])]
    pallas_call x1, Pallas kernels: 85.6 us -> 47.9 us  [on_device(): pl.pallas_call(functools.partial(cholesky_kernel, corner_place), out_shap...]
    ppermute x0 -> x10, starting transfers between devices: none -> 12.1 us  [gather_by_distance(): lax.ppermute(x, axis, [(i, (i + d) % count) for i in range(count)])]
  transfers between devices with their start and end apart: 5 -> 13, of which waited for: 3 -> 8; matrix products, arithmetic and copies ran while one was open for 1% -> 1% of each run, Pallas kernels for 37% -> 0%
where the time goes in v2:
time: 204 us; the launch traced here: 203 us
  waiting for transfers between devices  104 us (51%)
  Pallas kernels  62.9 us (31%)
  starting transfers between devices  15.6 us (8%)
  between operations  13.5 us (7%)
  other arithmetic  3.34 us (2%)
  local copies, waits for them, and re-layouts  2.32 us (1%)
    pallas_call x1, Pallas kernels, on_device(): pl.pallas_call(functools.partial(cholesky_kernel, corner_place), out_shap...  47.9 us
    all_gather x1, waiting for transfers between devices, on_device(): lax.all_gather(child_panels[0], 'front', axis=0, tiled=True)  45.1 us
    ppermute x10, waiting for transfers between devices, gather_by_distance(): lax.ppermute(x, axis, [(i, (i + d) % count) for i in range(count)])  37.8 us
    all_gather x1, waiting for transfers between devices, on_device(): corner = lax.all_gather(tops[0], ('leaf', 'front'), axis=0, tiled=True)  14.8 us
    ppermute x10, starting transfers between devices, gather_by_distance(): lax.ppermute(x, axis, [(i, (i + d) % count) for i in range(count)])  12.1 us
    pallas_call x1, Pallas kernels, on_device(): pl.pallas_call(functools.partial(solve_kernel, leaf_count, front_count, f...  11.7 us
    all_to_all x1, waiting for transfers between devices, on_device(): lax.all_to_all(update.reshape(spread, leaf_count, size, size), 'leaf', sp...  5.37 us
  transfers between devices with their start and end apart: 13, of which 8 were waited for; matrix products, arithmetic and copies ran while one was open for 1% of the time, Pallas kernels for 0%

profile of v2, /device:TPU:0, one launch (start us, length us, event | category | flops | bytes accessed | tf_op | source)
XLA Modules:
  0.0 203.2 jit_solution(8401000346784184827)
XLA Ops:
  6.5 0.7 all-gather.5.cloned.1.call-update
  7.3 45.1 %all-gather.5.cloned.1.call-done = bf16[1,1024,512]{2,1,0:T(8,128)(2,1)} async-done(((bf16[1,128,512]{2,1,0:T(8,128)(2,1)}), bf16[1,1024,512]{2,1,0:T(8,128)(2,1)}) %all-gather.5.cloned.1.call-update) | async-done | bytes 1048592 | tf_op jit(solution)/shard_map/all_gather | solution.py:234
  52.4 1.8 fusion
  54.1 0.7 copy.10
  54.9 3.4 %all-to-all-start = ((bf16[1,2,4,128,128]{4,3,1,0,2:T(8,128)(2,1)}), bf16[1,2,4,128,128]{4,3,1,0,2:T(8,128)(2,1)S(1)}, u32[]{:S(2)}, u32[]{:S(2)}) async-start(bf16[1,2,4,128,128]{4,3,1,0,2:T(8,128)(2,1)} %copy.10), calls=%async_computation | async-start | bytes 524288 | tf_op jit(solution)/shard_map/all_to_all | solution.py:240
  58.3 0.0 all-gather.7.cloned.1.call-start
  58.3 0.6 pad_add_fusion.where_ref
  58.9 5.4 %all-to-all-done = bf16[1,2,4,128,128]{4,3,1,0,2:T(8,128)(2,1)S(1)} async-done(((bf16[1,2,4,128,128]{4,3,1,0,2:T(8,128)(2,1)}), bf16[1,2,4,128,128]{4,3,1,0,2:T(8,128)(2,1)S(1)}, u32[]{:S(2)}, u32[]{:S(2)}) %all-to-all-start) | async-done | bytes 262176 | tf_op jit(solution)/shard_map/all_to_all | solution.py:240
  64.3 0.7 copy-done.1
  65.0 3.3 %shard_map.46.full_ref = f32[4,1024,128]{2,1,0:T(8,128)} custom-call(s32[2]{0:T(128)} %pad_add_fusion.where_ref, s32[4,8]{1,0:T(4,128)} %map_ref.1, bf16[4,2,128,128]{3,2,1,0:T(8,128)(2,1)} %bitcast.33, f32[4096,128]{1,0:T(8,128)} %bitcast.32), custom_call_target="tpu_custom_call" | custom-call | tf_op jit(solution)/shard_map/pallas_call | solution.py:243
  68.3 1.7 convert.5
  70.0 0.6 slice.15
  70.6 0.0 all-gather.7.cloned.1.call-update
  70.7 0.6 collective-permute-start
  71.3 0.5 collective-permute-start.1
  71.8 2.1 %collective-permute-start.3 = (bf16[768,128]{1,0:T(8,128)(2,1)S(1)}, bf16[768,128]{1,0:T(8,128)(2,1)S(1)}, u32[]{:S(2)}, u32[]{:S(2)}) collective-permute-start(bf16[768,128]{1,0:T(8,128)(2,1)S(1)} %slice_bitcast_fusion.1), channel_id=1, source_target_pairs={{0,4},{1,5},{2,6},{3,7},{4,0},{5,1},{6,2},{7,3},{8,12},{9,13},{10,... | collective-permute-start | bytes 589832 | tf_op jit(solution)/shard_map/ppermute | solution.py:218
  73.9 2.1 %collective-permute-start.4 = (bf16[768,128]{1,0:T(8,128)(2,1)S(1)}, bf16[768,128]{1,0:T(8,128)(2,1)S(1)}, u32[]{:S(2)}, u32[]{:S(2)}) collective-permute-start(bf16[768,128]{1,0:T(8,128)(2,1)S(1)} %slice_bitcast_fusion.1), channel_id=1, source_target_pairs={{0,5},{1,6},{2,7},{3,0},{4,1},{5,2},{6,3},{7,4},{8,13},{9,14},{10,... | collective-permute-start | bytes 589832 | tf_op jit(solution)/shard_map/ppermute | solution.py:218
  76.1 0.9 collective-permute-start.2
  77.0 4.5 %collective-permute-done = bf16[768,128]{1,0:T(8,128)(2,1)S(1)} collective-permute-done((bf16[768,128]{1,0:T(8,128)(2,1)S(1)}, bf16[768,128]{1,0:T(8,128)(2,1)S(1)}, u32[]{:S(2)}, u32[]{:S(2)}) %collective-permute-start) | collective-permute-done | bytes 196640 | tf_op jit(solution)/shard_map/ppermute | solution.py:218
  81.4 0.1 collective-permute-start.5
  81.6 4.1 %collective-permute-start.6 = (bf16[768,128]{1,0:T(8,128)(2,1)S(1)}, bf16[768,128]{1,0:T(8,128)(2,1)S(1)}, u32[]{:S(2)}, u32[]{:S(2)}) collective-permute-start(bf16[768,128]{1,0:T(8,128)(2,1)S(1)} %slice_bitcast_fusion.1), channel_id=1, source_target_pairs={{0,7},{1,0},{2,1},{3,2},{4,3},{5,4},{6,5},{7,6},{8,15},{9,8},{10,9... | collective-permute-start | bytes 589832 | tf_op jit(solution)/shard_map/ppermute | solution.py:218
  85.7 20.9 %collective-permute-done.2 = bf16[768,128]{1,0:T(8,128)(2,1)S(1)} collective-permute-done((bf16[768,128]{1,0:T(8,128)(2,1)S(1)}, bf16[768,128]{1,0:T(8,128)(2,1)S(1)}, u32[]{:S(2)}, u32[]{:S(2)}) %collective-permute-start.2) | collective-permute-done | bytes 196640 | tf_op jit(solution)/shard_map/ppermute | solution.py:218
  106.7 0.2 collective-permute-start.9
  106.9 1.5 collective-permute-start.8
  108.4 0.1 collective-permute-start.7
  108.6 4.8 %collective-permute-done.9 = bf16[256,512]{1,0:T(8,128)(2,1)S(1)} collective-permute-done((bf16[256,512]{1,0:T(8,128)(2,1)S(1)}, bf16[256,512]{1,0:T(8,128)(2,1)S(1)}, u32[]{:S(2)}, u32[]{:S(2)}) %collective-permute-start.9) | collective-permute-done | bytes 262176 | tf_op jit(solution)/shard_map/ppermute | solution.py:218
  113.4 7.5 %collective-permute-done.8 = bf16[256,512]{1,0:T(8,128)(2,1)S(1)} collective-permute-done((bf16[256,512]{1,0:T(8,128)(2,1)S(1)}, bf16[256,512]{1,0:T(8,128)(2,1)S(1)}, u32[]{:S(2)}, u32[]{:S(2)}) %collective-permute-start.8) | collective-permute-done | bytes 262176 | tf_op jit(solution)/shard_map/ppermute | solution.py:218
  120.9 0.1 collective-permute-done.7
  121.0 1.0 pad_maximum_fusion.tops_ref
  122.0 14.8 %all-gather.7.cloned.1.call-done = bf16[1,8192,128]{2,1,0:T(8,128)(2,1)} async-done(((bf16[1,256,128]{2,1,0:T(8,128)(2,1)}), bf16[1,8192,128]{2,1,0:T(8,128)(2,1)}) %all-gather.7.cloned.1.call-update) | async-done | bytes 2097168 | tf_op jit(solution)/shard_map/all_gather | solution.py:256
  136.8 47.9 %shard_map.47 = (f32[1024,1024]{1,0:T(8,128)}, f32[1024,128]{1,0:T(8,128)}) custom-call(bf16[8192,128]{1,0:T(8,128)(2,1)} %bitcast.35), custom_call_target="tpu_custom_call" | custom-call | flops 8589934592 | bytes 8388608 | tf_op jit(solution)/shard_map/pallas_call | solution.py:265
  184.7 11.7 %shard_map.48 = f32[4096,128]{1,0:T(8,128)} custom-call(s32[2]{0:T(128)} %pad_add_fusion.where_ref, f32[1024,1024]{1,0:T(8,128)} %get-tuple-element.7.l_ref, f32[1024,128]{1,0:T(8,128)} %get-tuple-element.8.z_ref, bf16[6144,128]{1,0:T(8,128)(2,1)} %copy-done, bf16[1024,512]{1,0:T(8,128)(2,1)} %pad_maximum_fusion.tops_ref, f32[4,1024,128]{2,1,0:T(8,128)} %shard_map.46.full_ref), custom_call_target="tpu_custom_call" | custom-call | tf_op jit(solution)/shard_map/pallas_call | solution.py:283
  (19 shorter events, 0.3 us)
Async XLA Ops:
  6.5 45.8 %all-gather.5.cloned.1.call-start = ((), (), s32[]{:S(2)}) async-start(), calls=%async_computation.1 | async-start | bytes 1179648 | tf_op jit(solution)/shard_map/all_gather | solution.py:234
  54.9 9.4 %all-to-all-start = ((bf16[1,2,4,128,128]{4,3,1,0,2:T(8,128)(2,1)}), bf16[1,2,4,128,128]{4,3,1,0,2:T(8,128)(2,1)S(1)}, u32[]{:S(2)}, u32[]{:S(2)}) async-start(bf16[1,2,4,128,128]{4,3,1,0,2:T(8,128)(2,1)} %copy.10), calls=%async_computation | async-start | bytes 524288 | tf_op jit(solution)/shard_map/all_to_all | solution.py:240
  58.3 78.5 %all-gather.7.cloned.1.call-start = ((), (), s32[]{:S(2)}) async-start(), calls=%async_computation.2 | async-start | bytes 2162688 | tf_op jit(solution)/shard_map/all_gather | solution.py:256
  64.3 0.7 copy-start.1
  70.7 10.8 %collective-permute-start = (bf16[768,128]{1,0:T(8,128)(2,1)S(1)}, bf16[768,128]{1,0:T(8,128)(2,1)S(1)}, u32[]{:S(2)}, u32[]{:S(2)}) collective-permute-start(bf16[768,128]{1,0:T(8,128)(2,1)S(1)} %slice_bitcast_fusion.1), channel_id=1, source_target_pairs={{0,1},{1,2},{2,3},{3,4},{4,5},{5,6},{6,7},{7,0},{8,9},{9,10},{10,1... | collective-permute-start | bytes 589832 | tf_op jit(solution)/shard_map/ppermute | solution.py:218
  71.3 10.3 %collective-permute-start.1 = (bf16[768,128]{1,0:T(8,128)(2,1)S(1)}, bf16[768,128]{1,0:T(8,128)(2,1)S(1)}, u32[]{:S(2)}, u32[]{:S(2)}) collective-permute-start(bf16[768,128]{1,0:T(8,128)(2,1)S(1)} %slice_bitcast_fusion.1), channel_id=1, source_target_pairs={{0,2},{1,3},{2,4},{3,5},{4,6},{5,7},{6,0},{7,1},{8,10},{9,11},{10,... | collective-permute-start | bytes 589832 | tf_op jit(solution)/shard_map/ppermute | solution.py:218
  71.8 35.0 %collective-permute-start.3 = (bf16[768,128]{1,0:T(8,128)(2,1)S(1)}, bf16[768,128]{1,0:T(8,128)(2,1)S(1)}, u32[]{:S(2)}, u32[]{:S(2)}) collective-permute-start(bf16[768,128]{1,0:T(8,128)(2,1)S(1)} %slice_bitcast_fusion.1), channel_id=1, source_target_pairs={{0,4},{1,5},{2,6},{3,7},{4,0},{5,1},{6,2},{7,3},{8,12},{9,13},{10,... | collective-permute-start | bytes 589832 | tf_op jit(solution)/shard_map/ppermute | solution.py:218
  73.9 34.4 %collective-permute-start.4 = (bf16[768,128]{1,0:T(8,128)(2,1)S(1)}, bf16[768,128]{1,0:T(8,128)(2,1)S(1)}, u32[]{:S(2)}, u32[]{:S(2)}) collective-permute-start(bf16[768,128]{1,0:T(8,128)(2,1)S(1)} %slice_bitcast_fusion.1), channel_id=1, source_target_pairs={{0,5},{1,6},{2,7},{3,0},{4,1},{5,2},{6,3},{7,4},{8,13},{9,14},{10,... | collective-permute-start | bytes 589832 | tf_op jit(solution)/shard_map/ppermute | solution.py:218
  76.1 30.6 %collective-permute-start.2 = (bf16[768,128]{1,0:T(8,128)(2,1)S(1)}, bf16[768,128]{1,0:T(8,128)(2,1)S(1)}, u32[]{:S(2)}, u32[]{:S(2)}) collective-permute-start(bf16[768,128]{1,0:T(8,128)(2,1)S(1)} %slice_bitcast_fusion.1), channel_id=1, source_target_pairs={{0,3},{1,4},{2,5},{3,6},{4,7},{5,0},{6,1},{7,2},{8,11},{9,12},{10,... | collective-permute-start | bytes 589832 | tf_op jit(solution)/shard_map/ppermute | solution.py:218
  81.4 27.0 %collective-permute-start.5 = (bf16[768,128]{1,0:T(8,128)(2,1)S(1)}, bf16[768,128]{1,0:T(8,128)(2,1)S(1)}, u32[]{:S(2)}, u32[]{:S(2)}) collective-permute-start(bf16[768,128]{1,0:T(8,128)(2,1)S(1)} %slice_bitcast_fusion.1), channel_id=1, source_target_pairs={{0,6},{1,7},{2,0},{3,1},{4,2},{5,3},{6,4},{7,5},{8,14},{9,15},{10,... | collective-permute-start | bytes 589832 | tf_op jit(solution)/shard_map/ppermute | solution.py:218
  81.6 27.0 %collective-permute-start.6 = (bf16[768,128]{1,0:T(8,128)(2,1)S(1)}, bf16[768,128]{1,0:T(8,128)(2,1)S(1)}, u32[]{:S(2)}, u32[]{:S(2)}) collective-permute-start(bf16[768,128]{1,0:T(8,128)(2,1)S(1)} %slice_bitcast_fusion.1), channel_id=1, source_target_pairs={{0,7},{1,0},{2,1},{3,2},{4,3},{5,4},{6,5},{7,6},{8,15},{9,8},{10,9... | collective-permute-start | bytes 589832 | tf_op jit(solution)/shard_map/ppermute | solution.py:218
  106.7 6.7 %collective-permute-start.9 = (bf16[256,512]{1,0:T(8,128)(2,1)S(1)}, bf16[256,512]{1,0:T(8,128)(2,1)S(1)}, u32[]{:S(2)}, u32[]{:S(2)}) collective-permute-start(bf16[256,512]{1,0:T(8,128)(2,1)S(1)} %copy_bitcast_fusion), channel_id=1, source_target_pairs={{0,24},{8,0},{16,8},{24,16},{1,25},{9,1},{17,9},{25,17},{2,26},{10... | collective-permute-start | bytes 786440 | tf_op jit(solution)/shard_map/ppermute | solution.py:218
  106.9 14.0 %collective-permute-start.8 = (bf16[256,512]{1,0:T(8,128)(2,1)S(1)}, bf16[256,512]{1,0:T(8,128)(2,1)S(1)}, u32[]{:S(2)}, u32[]{:S(2)}) collective-permute-start(bf16[256,512]{1,0:T(8,128)(2,1)S(1)} %copy_bitcast_fusion), channel_id=1, source_target_pairs={{0,16},{8,24},{16,0},{24,8},{1,17},{9,25},{17,1},{25,9},{2,18},{10... | collective-permute-start | bytes 786440 | tf_op jit(solution)/shard_map/ppermute | solution.py:218
  108.4 12.6 %collective-permute-start.7 = (bf16[256,512]{1,0:T(8,128)(2,1)S(1)}, bf16[256,512]{1,0:T(8,128)(2,1)S(1)}, u32[]{:S(2)}, u32[]{:S(2)}) collective-permute-start(bf16[256,512]{1,0:T(8,128)(2,1)S(1)} %copy_bitcast_fusion), channel_id=1, source_target_pairs={{0,8},{8,16},{16,24},{24,0},{1,9},{9,17},{17,25},{25,1},{2,10},{10... | collective-permute-start | bytes 786440 | tf_op jit(solution)/shard_map/ppermute | solution.py:218
  108.6 76.1 %copy-start = (bf16[6144,128]{1,0:T(8,128)(2,1)}, bf16[6144,128]{1,0:T(8,128)(2,1)S(1)}, u32[]{:S(2)}) copy-start(bf16[6144,128]{1,0:T(8,128)(2,1)S(1)} %constant_dynamic-update-slice_fusion.rows_ref) | copy-start | bytes 4718596
Sparse Core Ops, SparseCore 0:
  9.5 42.8 all-gather.4
  70.8 65.9 all-gather.6

commit v3 on v2

--- a/solution.py
+++ b/solution.py
@@ -159,7 +159,7 @@
 
 
 def solve_kernel(
-    leaf_count, front_count, first, where_ref, l_ref, z_ref, rows_ref, tops_ref, full_ref, out_ref, s_ref, w_ref
+    leaf_count, first, where_ref, l_ref, z_ref, rows_ref, tops_ref, full_ref, out_ref, s_ref, w_ref
 ):
     col_blocks, all_rows, size = full_ref.shape
     top = tops_ref.shape[0] // leaf_count // size
@@ -169,8 +169,7 @@
     for k in range(KS):
         at = slice(k * size, (k + 1) * size)
         inverse = z_ref[at, :].astype(low)
-        distance = lax.rem(front_id - k + front_count, front_count)
-        own = rows_ref[pl.ds(pl.multiple_of(distance * rows, size), rows), :]
+        own = rows_ref[k * rows : (k + 1) * rows, :]
         distance = lax.rem(leaf_id - k % leaf_count + leaf_count, leaf_count)
         source = (distance * top + k // leaf_count) * size
         met = tops_ref[pl.ds(pl.multiple_of(source, size), size), first * size :]
@@ -211,6 +210,217 @@
             complement(s)
 
 
+MESH = pl.DeviceIdType.MESH
+DMA = pltpu.SemaphoreType.DMA
+
+
+def ring_position(member, count):
+    side = lax.rem(member, 2)
+    step = lax.div(member, 2)
+    return step + side * (count - 1 - 2 * step)
+
+
+def ring_member(position, count):
+    side = lax.div(position, count // 2)
+    return 2 * (position + side * (count - 1 - 2 * position)) + side
+
+
+def behind(position, steps, count):
+    return lax.rem(position - steps + count, count)
+
+
+def ring_hops(position, count, first, slot, sems):
+    send, recv = sems
+    half = count // 2
+    rows = first.shape[0]
+    after = ring_member(lax.rem(position + 1, count), count)
+    ahead = ring_member(behind(position, 1, count), count)
+
+    def hop(way, s):
+        to = s if way == 0 else count - s
+        source = first if s == 1 else slot(to - 1 if way == 0 else to + 1)
+        target = slot(to)
+        if s == half:
+            part = pl.ds(0, rows // 2) if way == 0 else pl.ds(rows // 2, rows // 2)
+            source, target = source.at[part], target.at[part]
+        return pltpu.make_async_remote_copy(
+            src_ref=source,
+            dst_ref=target,
+            send_sem=send.at[way, s],
+            recv_sem=recv.at[way, s],
+            device_id={"front": after if way == 0 else ahead},
+            device_id_type=MESH,
+        )
+
+    return hop, (after, ahead)
+
+
+def ring_run(hop, half, ready):
+    for way in (0, 1):
+        hop(way, 1).start()
+    ready(0)
+    for s in range(1, half + 1):
+        for way in (0, 1):
+            hop(way, s).wait_recv()
+            if s < half:
+                hop(way, s + 1).start()
+        ready(s)
+        if s < half:
+            ready(2 * half - s)
+
+
+def ring_end(hop, half):
+    for s in range(1, half + 1):
+        for way in (0, 1):
+            hop(way, s).wait_send()
+
+
+def greet(barrier, devices):
+    for device in devices:
+        pl.semaphore_signal(barrier, inc=1, device_id=device, device_id_type=MESH)
+    pl.semaphore_wait(barrier, len(devices))
+
+
+def update_kernel(
+    leaf_count, front_count, panel_ref, blocks_ref, got_ref,
+    slots, stage, land, ring_send, ring_recv, out_send, out_recv,
+):
+    leaf_id, front_id = lax.axis_index("leaf"), lax.axis_index("front")
+    size = panel_ref.shape[0]
+    half = front_count // 2
+    position = ring_position(front_id, front_count)
+    hop, beside = ring_hops(
+        position, front_count, panel_ref, lambda s: slots.at[s], (ring_send, ring_recv)
+    )
+    greet(
+        pltpu.get_barrier_semaphore(),
+        [{"front": f} for f in beside]
+        + [{"leaf": lax.rem(leaf_id + d, leaf_count)} for d in range(1, leaf_count)],
+    )
+
+    def deliver(s):
+        block = ring_member(behind(position, s, front_count), front_count)
+        owner, turn = lax.rem(block, leaf_count), lax.div(block, leaf_count)
+        copy = pltpu.make_async_remote_copy(
+            src_ref=stage.at[s],
+            dst_ref=land.at[leaf_id, turn],
+            send_sem=out_send.at[s],
+            recv_sem=out_recv.at[leaf_id, turn],
+            device_id={"leaf": owner},
+            device_id_type=MESH,
+        )
+        return block, owner, turn, copy
+
+    def ready(s):
+        block, owner, turn, copy = deliver(s)
+        rows = panel_ref[...] if s == 0 else slots[s]
+        given = blocks_ref[pl.ds(pl.multiple_of(block * size, size), size), :]
+        product = dot(rows, panel_ref[...], NT)
+        value = (given.astype(jnp.float32) - product).astype(jnp.bfloat16)
+        stage[s] = value
+
+        @pl.when(owner == leaf_id)
+        def _():
+            land[leaf_id, turn] = value
+
+        @pl.when(owner != leaf_id)
+        def _():
+            copy.start()
+
+    ring_run(hop, half, ready)
+    for d in range(1, leaf_count):
+        source = lax.rem(leaf_id + d, leaf_count)
+        for turn in range(land.shape[1]):
+            pltpu.make_async_remote_copy(
+                src_ref=stage.at[0],
+                dst_ref=land.at[source, turn],
+                send_sem=out_send.at[0],
+                recv_sem=out_recv.at[source, turn],
+                device_id={"leaf": source},
+                device_id_type=MESH,
+            ).wait_recv()
+    got_ref[...] = land[...]
+    for s in range(front_count):
+        _, owner, _, copy = deliver(s)
+        pl.when(owner != leaf_id)(copy.wait_send)
+    ring_end(hop, half)
+
+
+def corner_kernel(
+    leaf_count, front_count, piece_ref, out_ref,
+    held, ring_send, ring_recv, far_send, far_recv, near_send, near_recv,
+):
+    leaf_id, front_id = lax.axis_index("leaf"), lax.axis_index("front")
+    rows = piece_ref.shape[0]
+    half = front_count // 2
+    chips = leaf_count // 2
+    chip, core = lax.div(leaf_id, 2), lax.rem(leaf_id, 2)
+    mate = leaf_id + 1 - 2 * core
+    position = ring_position(front_id, front_count)
+    hop, beside = ring_hops(
+        position,
+        front_count,
+        piece_ref,
+        lambda s: held.at[leaf_id, s],
+        (ring_send, ring_recv),
+    )
+    greet(
+        pltpu.get_barrier_semaphore(),
+        [{"front": f} for f in beside]
+        + [{"leaf": 2 * lax.rem(chip + d, chips) + core} for d in range(1, chips)]
+        + [{"leaf": mate}],
+    )
+
+    def far(d, s, source):
+        return pltpu.make_async_remote_copy(
+            src_ref=held.at[source, s],
+            dst_ref=held.at[source, s],
+            send_sem=far_send.at[d - 1, s],
+            recv_sem=far_recv.at[d - 1, s],
+            device_id={"leaf": 2 * lax.rem(chip + d, chips) + core},
+            device_id_type=MESH,
+        )
+
+    def near(d, s, source):
+        return pltpu.make_async_remote_copy(
+            src_ref=held.at[source, s],
+            dst_ref=held.at[source, s],
+            send_sem=near_send.at[d, s],
+            recv_sem=near_recv.at[d, s],
+            device_id={"leaf": mate},
+            device_id_type=MESH,
+        )
+
+    held[leaf_id, 0] = piece_ref[...]
+
+    def ready(s):
+        for d in range(1, chips):
+            far(d, s, leaf_id).start()
+        near(0, s, leaf_id).start()
+
+    ring_run(hop, half, ready)
+    order = [0] + [t for s in range(1, half) for t in (s, front_count - s)] + [half]
+    for s in order:
+        for d in range(1, chips):
+            source = 2 * behind(chip, d, chips) + core
+            far(d, s, source).wait_recv()
+            near(d, s, source).start()
+    for s in order:
+        for d in range(chips):
+            near(d, s, 2 * behind(chip, d, chips) + 1 - core).wait_recv()
+    for s in range(front_count):
+        column = ring_member(behind(position, s, front_count), front_count)
+        for source in range(leaf_count):
+            at = pl.multiple_of((source * front_count + column) * rows, rows)
+            out_ref[pl.ds(at, rows), :] = held[source, s]
+    for s in range(front_count):
+        for d in range(1, chips):
+            far(d, s, leaf_id).wait_send()
+        for d in range(chips):
+            near(d, s, leaf_id).wait_send()
+    ring_end(hop, half)
+
+
 def gather_by_distance(x, axis):
     count = lax.axis_size(axis)
     pieces = [x]
@@ -230,16 +440,25 @@
     top = KS // leaf_count
     first = KS // front_count
     params = pltpu.CompilerParams(vmem_limit_bytes=LIMIT)
-    product = lax.dot_general(
-        lax.all_gather(child_panels[0], "front", axis=0, tiled=True),
-        child_panels[0],
-        NT,
-        preferred_element_type=jnp.float32,
-    )
-    update = (child_blocks[0].astype(jnp.float32) - product).astype(jnp.bfloat16)
-    got = lax.all_to_all(
-        update.reshape(spread, leaf_count, size, size), "leaf", split_axis=1, concat_axis=0
-    )
+    piv = child_panels.shape[2]
+    half = front_count // 2
+    ring = [DMA((2, half + 1)), DMA((2, half + 1))]
+    got = pl.pallas_call(
+        functools.partial(update_kernel, leaf_count, front_count),
+        out_shape=jax.ShapeDtypeStruct((children, spread, size, size), jnp.bfloat16),
+        in_specs=[VMEM, VMEM],
+        out_specs=VMEM,
+        scratch_shapes=[
+            pltpu.VMEM((front_count, size, piv), jnp.bfloat16),
+            pltpu.VMEM((front_count, size, size), jnp.bfloat16),
+            pltpu.VMEM((children, spread, size, size), jnp.bfloat16),
+        ]
+        + ring
+        + [DMA((front_count,)), DMA((children, spread))],
+        compiler_params=pltpu.CompilerParams(
+            vmem_limit_bytes=LIMIT, collective_id=0, has_side_effects=True
+        ),
+    )(child_panels[0], child_blocks[0])
     full = pl.pallas_call(
         functools.partial(assemble_kernel, leaf_count, front_count),
         out_shape=jax.ShapeDtypeStruct((col_blocks, rows, size), jnp.float32),
@@ -249,13 +468,30 @@
     )(
         place,
         child_map,
-        got.reshape(children, spread, size, size),
+        got,
         front_entries.reshape(rows * col_blocks, size),
     )
     tops = full[:, : top * size].astype(jnp.bfloat16)
-    corner = lax.all_gather(tops[0], ("leaf", "front"), axis=0, tiled=True)
-    below = gather_by_distance(full[0, top * size :].astype(jnp.bfloat16), "front")
+    chips = leaf_count // 2
+    corner = pl.pallas_call(
+        functools.partial(corner_kernel, leaf_count, front_count),
+        out_shape=jax.ShapeDtypeStruct(
+            (leaf_count * front_count * top * size, size), jnp.bfloat16
+        ),
+        in_specs=[VMEM],
+        out_specs=VMEM,
+        scratch_shapes=[pltpu.VMEM((leaf_count, front_count, top * size, size), jnp.bfloat16)]
+        + ring
+        + [DMA((max(chips - 1, 1), front_count))] * 2
+        + [DMA((chips, front_count))] * 2,
+        compiler_params=pltpu.CompilerParams(
+            vmem_limit_bytes=LIMIT, collective_id=1, has_side_effects=True
+        ),
+    )(tops[0])
+    below = full[0, top * size :].astype(jnp.bfloat16)
     across = jnp.swapaxes(tops, 0, 1).reshape(top * size, col_blocks * size)
+    corner, below, across = lax.optimization_barrier((corner, below, across))
+    below = lax.all_gather(below, "front", axis=0, tiled=True)
     across = gather_by_distance(across, "leaf")
     width = KS * size
 
@@ -281,7 +517,7 @@
         ),
     )(corner)
     result = pl.pallas_call(
-        functools.partial(solve_kernel, leaf_count, front_count, first),
+        functools.partial(solve_kernel, leaf_count, first),
         out_shape=jax.ShapeDtypeStruct((rows * col_blocks, size), jnp.float32),
         in_specs=[SMEM] + [VMEM] * 5,
         out_specs=VMEM,

time: 204 us -> 132 us (0.65)
  waiting for transfers between devices: 104 us -> 0.03 us
  Pallas kernels: 62.9 us -> 111 us
  starting transfers between devices: 15.6 us -> 2.21 us
    all_gather x2 -> x1, waiting for transfers between devices: 59.9 us -> 0.01 us  [on_device(): below = lax.all_gather(below, 'front', axis=0, tiled=True)]
    pallas_call x1 -> x3, Pallas kernels: 11.7 us -> 60.1 us  [the longest x1 25.8 us: on_device(): pl.pallas_call(functools.partial(update_kernel, leaf_count, front_count),...]
    ppermute x10 -> x3, waiting for transfers between devices: 37.8 us -> 0.01 us  [gather_by_distance(): lax.ppermute(x, axis, [(i, (i + d) % count) for i in range(count)])]
    ppermute x10 -> x3, starting transfers between devices: 12.1 us -> 2.21 us  [gather_by_distance(): lax.ppermute(x, axis, [(i, (i + d) % count) for i in range(count)])]
    all_to_all x1 -> x0, waiting for transfers between devices: 5.37 us -> none  [on_device(): lax.all_to_all(update.reshape(spread, leaf_count, size, size), 'leaf', sp...]
    all_to_all x1 -> x0, starting transfers between devices: 3.41 us -> none  [on_device(): lax.all_to_all(update.reshape(spread, leaf_count, size, size), 'leaf', sp...]
  transfers between devices with their start and end apart: 13 -> 4, of which waited for: 8 -> 0; matrix products, arithmetic and copies ran while one was open for 1% -> 1% of each run, Pallas kernels for 0% -> 36%
where the time goes in v3:
time: 132 us
  Pallas kernels  111 us (84%)
  between operations  13.4 us (10%)
  other arithmetic  3.37 us (3%)
  starting transfers between devices  2.21 us (2%)
  local copies, waits for them, and re-layouts  1.36 us (1%)
    pallas_call x1, Pallas kernels, on_device(): pl.pallas_call(functools.partial(cholesky_kernel, corner_place), out_shap...  47.9 us
    pallas_call x1, Pallas kernels, on_device(): pl.pallas_call(functools.partial(update_kernel, leaf_count, front_count),...  25.8 us
    pallas_call x1, Pallas kernels, on_device(): pl.pallas_call(functools.partial(corner_kernel, leaf_count, front_count),...  22.6 us
    pallas_call x1, Pallas kernels, on_device(): pl.pallas_call(functools.partial(solve_kernel, leaf_count, first), out_sh...  11.7 us
    pallas_call x1, Pallas kernels, on_device(): pl.pallas_call(functools.partial(assemble_kernel, leaf_count, front_count...  3.26 us
  transfers between devices with their start and end apart: 4, of which 0 were waited for; matrix products, arithmetic and copies ran while one was open for 1% of the time, Pallas kernels for 36%

profile of v3, /device:TPU:0, one launch (start us, length us, event | category | flops | bytes accessed | tf_op | source)
XLA Modules:
  0.0 131.6 jit_solution(13114177156131022513)
XLA Ops:
  6.5 0.0 all-gather.2.cloned.1.call-start
  6.5 0.6 pad_add_fusion.where_ref
  7.1 25.8 %shard_map.46.got_ref = bf16[4,2,128,128]{3,2,1,0:T(8,128)(2,1)} custom-call(bf16[128,512]{1,0:T(8,128)(2,1)} %bitcast.20, bf16[1024,128]{1,0:T(8,128)(2,1)} %bitcast.19), custom_call_target="tpu_custom_call" | custom-call | tf_op jit(solution)/shard_map/pallas_call | solution.py:446
  32.9 3.3 %shard_map.47.full_ref = f32[4,1024,128]{2,1,0:T(8,128)} custom-call(s32[2]{0:T(128)} %pad_add_fusion.where_ref, s32[4,8]{1,0:T(4,128)} %map_ref.1, bf16[4,2,128,128]{3,2,1,0:T(8,128)(2,1)} %shard_map.46.got_ref, f32[4096,128]{1,0:T(8,128)} %bitcast.18), custom_call_target="tpu_custom_call" | custom-call | tf_op jit(solution)/shard_map/pallas_call | solution.py:462
  36.2 1.7 %convert.4 = bf16[4,1024,128]{2,1,0:T(8,128)(2,1)S(1)} convert(f32[4,1024,128]{2,1,0:T(8,128)} %shard_map.47.full_ref) | non-fusion elementwise | flops 524288 | bytes 3145728 | tf_op jit(solution)/shard_map/convert.1
  37.9 0.6 slice_bitcast_fusion.2.piece_ref
  38.6 0.7 slice_bitcast_fusion.1
  39.2 22.6 %shard_map.48.blocks_ref = bf16[8192,128]{1,0:T(8,128)(2,1)} custom-call(bf16[256,128]{1,0:T(8,128)(2,1)} %slice_bitcast_fusion.2.piece_ref), custom_call_target="tpu_custom_call" | custom-call | tf_op jit(solution)/shard_map/pallas_call | solution.py:476
  61.9 0.0 all-gather.2.cloned.1.call-update
  61.9 0.6 collective-permute-start
  62.5 0.7 collective-permute-start.1
  63.2 0.9 collective-permute-start.2
  64.1 47.9 %shard_map.49 = (f32[1024,1024]{1,0:T(8,128)}, f32[1024,128]{1,0:T(8,128)}) custom-call(bf16[8192,128]{1,0:T(8,128)(2,1)} %shard_map.48.blocks_ref), custom_call_target="tpu_custom_call" | custom-call | flops 8589934592 | bytes 8388608 | tf_op jit(solution)/shard_map/pallas_call | solution.py:501
  112.0 0.0 collective-permute-done
  112.0 0.0 collective-permute-done.1
  112.0 0.0 collective-permute-done.2
  112.0 1.1 pad_maximum_fusion.tops_ref
  113.1 0.0 all-gather.2.cloned.1.call-done.rows_ref
  113.1 11.7 %shard_map.50 = f32[4096,128]{1,0:T(8,128)} custom-call(s32[2]{0:T(128)} %pad_add_fusion.where_ref, f32[1024,1024]{1,0:T(8,128)} %get-tuple-element.11.l_ref, f32[1024,128]{1,0:T(8,128)} %get-tuple-element.12.z_ref, bf16[6144,128]{1,0:T(8,128)(2,1)} %all-gather.2.cloned.1.call-done.rows_ref, bf16[1024,512]{1,0:T(8,128)(2,1)} %pad_maximum_fusion.tops_ref, ...), custom_call_target="tpu_custom_call" | custom-call | tf_op jit(solution)/shard_map/pallas_call | solution.py:519
  (1 shorter events, 0.0 us)
Async XLA Ops:
  6.5 106.5 %all-gather.2.cloned.1.call-start = ((), (), s32[]{:S(2)}) async-start(), calls=%async_computation | async-start | bytes 1769472 | tf_op jit(solution)/shard_map/all_gather | solution.py:494
  61.9 50.1 %collective-permute-start = (bf16[256,512]{1,0:T(8,128)(2,1)S(1)}, bf16[256,512]{1,0:T(8,128)(2,1)S(1)}, u32[]{:S(2)}, u32[]{:S(2)}) collective-permute-start(bf16[256,512]{1,0:T(8,128)(2,1)S(1)} %copy_bitcast_fusion), channel_id=1, source_target_pairs={{0,8},{8,16},{16,24},{24,0},{1,9},{9,17},{17,25},{25,1},{2,10},{10... | collective-permute-start | bytes 786440 | tf_op jit(solution)/shard_map/ppermute | solution.py:428
  62.5 49.5 %collective-permute-start.1 = (bf16[256,512]{1,0:T(8,128)(2,1)S(1)}, bf16[256,512]{1,0:T(8,128)(2,1)S(1)}, u32[]{:S(2)}, u32[]{:S(2)}) collective-permute-start(bf16[256,512]{1,0:T(8,128)(2,1)S(1)} %copy_bitcast_fusion), channel_id=1, source_target_pairs={{0,16},{8,24},{16,0},{24,8},{1,17},{9,25},{17,1},{25,9},{2,18},{10... | collective-permute-start | bytes 786440 | tf_op jit(solution)/shard_map/ppermute | solution.py:428
  63.2 48.8 %collective-permute-start.2 = (bf16[256,512]{1,0:T(8,128)(2,1)S(1)}, bf16[256,512]{1,0:T(8,128)(2,1)S(1)}, u32[]{:S(2)}, u32[]{:S(2)}) collective-permute-start(bf16[256,512]{1,0:T(8,128)(2,1)S(1)} %copy_bitcast_fusion), channel_id=1, source_target_pairs={{0,24},{8,0},{16,8},{24,16},{1,25},{9,1},{17,9},{25,17},{2,26},{10... | collective-permute-start | bytes 786440 | tf_op jit(solution)/shard_map/ppermute | solution.py:428
Sparse Core Ops, SparseCore 0:
  62.0 42.5 all-gather.1

commit v4 on v3

--- a/solution.py
+++ b/solution.py
@@ -28,28 +28,33 @@
     return dot(a[0], b[0], dims) + (dot(a[0], b[1], dims) + dot(a[1], b[0], dims))
 
 
-def factor_block(a_ref, u_ref, z_ref):
-    size = a_ref.shape[0]
+def factor_half(a_ref, u_ref):
+    size, width = a_ref.shape
     tiles = size // 8
-    sub = lax.broadcasted_iota(jnp.int32, (8, size), 0)
-    lane = lax.broadcasted_iota(jnp.int32, (8, size), 1)
-    a = [a_ref[8 * t : 8 * t + 8, :] for t in range(tiles)]
-    z = [jnp.where(lane == sub + 8 * t, 1.0, 0.0).astype(jnp.float32) for t in range(tiles)]
+    sub = lax.broadcasted_iota(jnp.int32, (8, width), 0)
+    lane = lax.broadcasted_iota(jnp.int32, (8, width), 1)
+    a = [
+        jnp.where(
+            lane < size,
+            a_ref[8 * t : 8 * t + 8, :],
+            jnp.where(lane == sub + (size + 8 * t), 1.0, 0.0),
+        )
+        for t in range(tiles)
+    ]
 
     def row(tile, s):
-        return jnp.broadcast_to(tile[s : s + 1, :], (8, size))
+        return jnp.broadcast_to(tile[s : s + 1, :], (8, width))
 
     def column(tile, j):
-        return jnp.broadcast_to(tile[:, j : j + 1], (8, size))
+        return jnp.broadcast_to(tile[:, j : j + 1], (8, width))
 
     for t0 in range(tiles):
         base = 8 * t0
         spread = [column(a[t0], base + k) for k in range(8)]
         e = {(m, k): row(spread[k], m) for k in range(8) for m in range(k + 1)}
         r = [row(a[t0], m) for m in range(8)]
-        q = [row(z[t0], m) for m in range(8)]
         x = {t: [column(a[t], base + k) for k in range(8)] for t in range(t0 + 1, tiles)}
-        w, v, solved = [None] * 8, [None] * 8, {}
+        w, solved = [None] * 8, {}
         for j in range(0, 8, 2):
             p00, p01, p11 = e[j, j], e[j, j + 1], e[j + 1, j + 1]
             det = p00 * p11 - p01 * p01
@@ -66,40 +71,55 @@
                 for k in range(m, 8):
                     e[m, k] = e[m, k] - (e[j, m] * solved[j, k] + e[j + 1, m] * solved[j + 1, k])
             w[j], w[j + 1] = pivot(r[j], r[j + 1])
-            v[j], v[j + 1] = pivot(q[j], q[j + 1])
             for m in range(j + 2, 8):
                 r[m] = r[m] - (e[j, m] * w[j] + e[j + 1, m] * w[j + 1])
-                q[m] = q[m] - (e[j, m] * v[j] + e[j + 1, m] * v[j + 1])
             d0 = lax.rsqrt(p00)
             ratio = p01 * d0 * d0
             d1 = lax.rsqrt(p11 - ratio * p01)
             at = base + j
             u_ref[at : at + 1, :] = (r[j] * d0)[:1]
             u_ref[at + 1 : at + 2, :] = ((r[j + 1] - ratio * r[j]) * d1)[:1]
-            z_ref[at : at + 1, :] = (q[j] * d0)[:1]
-            z_ref[at + 1 : at + 2, :] = ((q[j + 1] - ratio * q[j]) * d1)[:1]
         if t0 + 1 == tiles:
             break
         for j in (4, 2, 0):
             for i in (j, j + 1):
                 for k in range(j + 2, 8):
                     w[i] = w[i] - solved[i, k] * w[k]
-                    v[i] = v[i] - solved[i, k] * v[k]
         for t in range(t0 + 1, tiles):
-            y = x[t]
-            terms = [y[k] * w[k] for k in range(8)]
+            terms = [x[t][k] * w[k] for k in range(8)]
             a[t] = a[t] - (
                 ((terms[0] + terms[1]) + (terms[2] + terms[3]))
                 + ((terms[4] + terms[5]) + (terms[6] + terms[7]))
             )
-            terms = [y[k] * v[k] for k in range(8)]
-            z[t] = z[t] - (
-                ((terms[0] + terms[1]) + (terms[2] + terms[3]))
-                + ((terms[4] + terms[5]) + (terms[6] + terms[7]))
-            )
-
-
-def cholesky_kernel(place, blocks_ref, l_ref, z_ref, a_ref, d_ref, u_ref):
+
+
+def factor_block(d_ref, l_ref, z_ref, h_ref, u_ref):
+    size = d_ref.shape[0]
+    half = size // 2
+    keep = lax.broadcasted_iota(jnp.int32, (half, half), 0) >= lax.broadcasted_iota(
+        jnp.int32, (half, half), 1
+    )
+    empty = jnp.zeros((half, half), jnp.float32)
+    factor_half(d_ref.at[:half, :], u_ref)
+    z1 = halves(u_ref[:, half:])
+    l_ref[:half, :half] = jnp.where(keep, u_ref[:, :half].T, 0.0)
+    z_ref[:half, :half] = u_ref[:, half:]
+    l21 = dot3(halves(d_ref[half:, :half]), z1, NT)
+    part = halves(l21)
+    h_ref[:, :half] = d_ref[half:, half:] - dot3(part, part, NT)
+    l_ref[half:, :half] = l21
+    l_ref[:half, half:] = empty
+    z_ref[:half, half:] = empty
+    cross = halves(dot3(part, z1, NN))
+    factor_half(h_ref, u_ref)
+    l_ref[half:, half:] = jnp.where(keep, u_ref[:, :half].T, 0.0)
+    z_ref[half:, half:] = u_ref[:, half:]
+    z_ref[half:, :half] = -dot3(halves(u_ref[:, half:]), cross, NN)
+
+
+def cholesky_kernel(
+    place, where_ref, blocks_ref, l_ref, z_ref, own_ref, a_ref, d_ref, f_ref, i_ref, h_ref, u_ref
+):
     size = blocks_ref.shape[1]
     for j in range(KS):
         for i in range(j, KS):
@@ -107,29 +127,32 @@
             a_ref[i * size : (i + 1) * size, j * size : (j + 1) * size] = blocks_ref[
                 at * size : (at + 1) * size, :
             ].astype(jnp.float32)
-            if i > j:
-                l_ref[j * size : (j + 1) * size, i * size : (i + 1) * size] = jnp.zeros(
-                    (size, size), jnp.float32
-                )
     d_ref[...] = a_ref[:size, :size]
-    keep = lax.broadcasted_iota(jnp.int32, (size, size), 0) >= lax.broadcasted_iota(
-        jnp.int32, (size, size), 1
-    )
+    h_ref[...] = jnp.zeros_like(h_ref)
 
     def step(k, carry):
-        z_now = z_ref.at[pl.ds(pl.multiple_of(k * size, size), size), :]
-        factor_block(d_ref, u_ref, z_now)
-        for now in range(KS):
+        factor_block(d_ref, f_ref, i_ref, h_ref, u_ref)
+        begin = pl.multiple_of(k * size, size)
+        z_ref[pl.ds(begin, size), :] = i_ref[...].astype(z_ref.dtype)
+
+        @pl.when(where_ref[1] == k)
+        def _():
+            own_ref[...] = jnp.zeros_like(own_ref)
+            own_ref[pl.ds(begin, size), :] = f_ref[...]
+
+        for now in range(KS - 1):
 
             @pl.when(k == now)
             def _():
                 low, high = now * size, (now + 1) * size
-                l_ref[low:high, low:high] = jnp.where(keep, u_ref[...].T, 0.0)
-                if now + 1 == KS:
-                    return
-                panel = dot3(halves(a_ref[high:, low:high]), halves(z_now[...]), NT)
-                l_ref[high:, low:high] = panel
+                panel = dot3(halves(a_ref[high:, low:high]), halves(i_ref[...]), NT)
                 parts = halves(panel)
+                l_ref[high:, low:high] = parts[0]
+
+                @pl.when(where_ref[1] == now)
+                def _():
+                    own_ref[high:, :] = panel
+
                 for j in range(now + 1, KS):
                     skip = (j - now - 1) * size
                     left = tuple(x[skip:] for x in parts)
@@ -145,7 +168,10 @@
     lax.fori_loop(0, KS, step, 0)
 
 
-def assemble_kernel(leaf_count, front_count, where_ref, map_ref, got_ref, front_ref, out_ref):
+def assemble_kernel(
+    leaf_count, front_count, where_ref, map_ref, got_ref, front_ref,
+    out_ref, piece_ref, across_ref, below_ref,
+):
     children, spread, size, _ = got_ref.shape
     leaf_id, front_id = where_ref[0], where_ref[1]
     rows = out_ref.shape[1]
@@ -156,10 +182,16 @@
         for q in range(spread):
             at = pl.multiple_of(map_ref[c, leaf_id + leaf_count * q] // leaf_count * size, size)
             out_ref[col, pl.ds(at, size), :] += got_ref[c, q].astype(jnp.float32)
+    top = piece_ref.shape[0]
+    piece_ref[...] = out_ref[0, :top, :].astype(jnp.bfloat16)
+    below_ref[...] = out_ref[0, top:, :].astype(jnp.bfloat16)
+    for s in range(out_ref.shape[0]):
+        across_ref[:, s * size : (s + 1) * size] = out_ref[s, :top, :].astype(jnp.bfloat16)
 
 
 def solve_kernel(
-    leaf_count, first, where_ref, l_ref, z_ref, rows_ref, tops_ref, full_ref, out_ref, s_ref, w_ref
+    leaf_count, first, where_ref, l_ref, z_ref, own_ref, rows_ref, tops_ref, full_ref,
+    out_ref, s_ref, w_ref,
 ):
     col_blocks, all_rows, size = full_ref.shape
     top = tops_ref.shape[0] // leaf_count // size
@@ -168,13 +200,13 @@
     low = jnp.bfloat16
     for k in range(KS):
         at = slice(k * size, (k + 1) * size)
-        inverse = z_ref[at, :].astype(low)
+        inverse = z_ref[at, :]
         own = rows_ref[k * rows : (k + 1) * rows, :]
         distance = lax.rem(leaf_id - k % leaf_count + leaf_count, leaf_count)
         source = (distance * top + k // leaf_count) * size
         met = tops_ref[pl.ds(pl.multiple_of(source, size), size), first * size :]
         if k:
-            before = l_ref[at, : k * size].astype(low)
+            before = l_ref[at, : k * size]
             own = (own.astype(jnp.float32) - dot(s_ref[:, : k * size], before, NT)).astype(low)
             met = (met.astype(jnp.float32) - dot(before, w_ref[: k * size, :], NN)).astype(low)
         solved = dot(own, inverse, NT)
@@ -186,8 +218,8 @@
             out_ref[pl.ds(top * size * col_blocks, rows, stride=col_blocks), :] = solved
             for t in range(top):
                 from_row = pl.multiple_of((t * leaf_count + leaf_id) * size, size)
-                out_ref[pl.ds(t * size * col_blocks, size, stride=col_blocks), :] = l_ref[
-                    pl.ds(from_row, size), at
+                out_ref[pl.ds(t * size * col_blocks, size, stride=col_blocks), :] = own_ref[
+                    pl.ds(from_row, size), :
                 ]
 
     def complement(s):
@@ -459,11 +491,16 @@
             vmem_limit_bytes=LIMIT, collective_id=0, has_side_effects=True
         ),
     )(child_panels[0], child_blocks[0])
-    full = pl.pallas_call(
+    full, piece, across, below = pl.pallas_call(
         functools.partial(assemble_kernel, leaf_count, front_count),
-        out_shape=jax.ShapeDtypeStruct((col_blocks, rows, size), jnp.float32),
+        out_shape=[
+            jax.ShapeDtypeStruct((col_blocks, rows, size), jnp.float32),
+            jax.ShapeDtypeStruct((top * size, size), jnp.bfloat16),
+            jax.ShapeDtypeStruct((top * size, col_blocks * size), jnp.bfloat16),
+            jax.ShapeDtypeStruct((rows - top * size, size), jnp.bfloat16),
+        ],
         in_specs=[SMEM, SMEM, VMEM, VMEM],
-        out_specs=VMEM,
+        out_specs=[VMEM] * 4,
         compiler_params=params,
     )(
         place,
@@ -471,7 +508,6 @@
         got,
         front_entries.reshape(rows * col_blocks, size),
     )
-    tops = full[:, : top * size].astype(jnp.bfloat16)
     chips = leaf_count // 2
     corner = pl.pallas_call(
         functools.partial(corner_kernel, leaf_count, front_count),
@@ -487,9 +523,7 @@
         compiler_params=pltpu.CompilerParams(
             vmem_limit_bytes=LIMIT, collective_id=1, has_side_effects=True
         ),
-    )(tops[0])
-    below = full[0, top * size :].astype(jnp.bfloat16)
-    across = jnp.swapaxes(tops, 0, 1).reshape(top * size, col_blocks * size)
+    )(piece)
     corner, below, across = lax.optimization_barrier((corner, below, across))
     below = lax.all_gather(below, "front", axis=0, tiled=True)
     across = gather_by_distance(across, "leaf")
@@ -498,35 +532,34 @@
     def corner_place(i, j):
         return ((i % leaf_count) * front_count + j) * top + i // leaf_count
 
-    lower, inverses = pl.pallas_call(
+    lower, inverses, column = pl.pallas_call(
         functools.partial(cholesky_kernel, corner_place),
         out_shape=[
-            jax.ShapeDtypeStruct((width, width), jnp.float32),
+            jax.ShapeDtypeStruct((width, width), jnp.bfloat16),
+            jax.ShapeDtypeStruct((width, size), jnp.bfloat16),
             jax.ShapeDtypeStruct((width, size), jnp.float32),
         ],
-        in_specs=[VMEM],
-        out_specs=[VMEM, VMEM],
-        scratch_shapes=[
-            pltpu.VMEM((width, width), jnp.float32),
-            pltpu.VMEM((size, size), jnp.float32),
-            pltpu.VMEM((size, size), jnp.float32),
-        ],
+        in_specs=[SMEM, VMEM],
+        out_specs=[VMEM] * 3,
+        scratch_shapes=[pltpu.VMEM((width, width), jnp.float32)]
+        + [pltpu.VMEM((size, size), jnp.float32)] * 3
+        + [pltpu.VMEM((size // 2, size), jnp.float32)] * 2,
         compiler_params=params,
         cost_estimate=pl.CostEstimate(
             flops=8 * width**3, bytes_accessed=8 * width * width, transcendentals=0
         ),
-    )(corner)
+    )(place, corner)
     result = pl.pallas_call(
         functools.partial(solve_kernel, leaf_count, first),
         out_shape=jax.ShapeDtypeStruct((rows * col_blocks, size), jnp.float32),
-        in_specs=[SMEM] + [VMEM] * 5,
+        in_specs=[SMEM] + [VMEM] * 6,
         out_specs=VMEM,
         scratch_shapes=[
             pltpu.VMEM((rows - top * size, width), jnp.bfloat16),
             pltpu.VMEM((width, (col_blocks - first) * size), jnp.bfloat16),
         ],
         compiler_params=params,
-    )(place, lower, inverses, below, across, full)
+    )(place, lower, inverses, column, below, across, full)
     return result.reshape(row_blocks, 1, size, col_blocks, 1, size)
 
 

time: 132 us -> 132 us (level)
  Pallas kernels: 111 us -> 115 us
  other arithmetic: 3.37 us -> 1.59 us
  local copies, waits for them, and re-layouts: 1.36 us -> 0.01 us
    pallas_call x1, Pallas kernels: 47.9 us -> 51.7 us  [on_device(): pl.pallas_call(functools.partial(cholesky_kernel, corner_place), out_shap...]
    another operation x1 -> x0, other arithmetic: 1.73 us -> none
  transfers between devices with their start and end apart: 4 -> 4, of which waited for: 0 -> 0; matrix products, arithmetic and copies ran while one was open for 1% -> 1% of each run, Pallas kernels for 36% -> 39%
where the time goes in v4:
time: 132 us
  Pallas kernels  115 us (87%)
  between operations  13.4 us (10%)
  starting transfers between devices  2.21 us (2%)
  other arithmetic  1.59 us (1%)
    pallas_call x1, Pallas kernels, on_device(): pl.pallas_call(functools.partial(cholesky_kernel, corner_place), out_shap...  51.7 us
    pallas_call x1, Pallas kernels, on_device(): pl.pallas_call(functools.partial(update_kernel, leaf_count, front_count),...  25.8 us
    pallas_call x1, Pallas kernels, on_device(): pl.pallas_call(functools.partial(corner_kernel, leaf_count, front_count),...  22.6 us
    pallas_call x1, Pallas kernels, on_device(): pl.pallas_call(functools.partial(solve_kernel, leaf_count, first), out_sh...  11.1 us
    pallas_call x1, Pallas kernels, on_device(): pl.pallas_call(functools.partial(assemble_kernel, leaf_count, front_count...  3.42 us
  transfers between devices with their start and end apart: 4, of which 0 were waited for; matrix products, arithmetic and copies ran while one was open for 1% of the time, Pallas kernels for 39%

profile of v4, /device:TPU:0, one launch (start us, length us, event | category | flops | bytes accessed | tf_op | source)
XLA Modules:
  0.0 131.9 jit_solution(10664128589249752468)
XLA Ops:
  6.5 0.0 all-gather.2.cloned.1.call-start
  6.5 0.6 pad_add_fusion.where_ref
  7.1 25.8 %shard_map.46.got_ref = bf16[4,2,128,128]{3,2,1,0:T(8,128)(2,1)} custom-call(bf16[128,512]{1,0:T(8,128)(2,1)} %bitcast.10, bf16[1024,128]{1,0:T(8,128)(2,1)} %bitcast.9), custom_call_target="tpu_custom_call" | custom-call | tf_op jit(solution)/shard_map/pallas_call | solution.py:478
  32.9 3.4 %shard_map.47 = (f32[4,1024,128]{2,1,0:T(8,128)}, bf16[256,128]{1,0:T(8,128)(2,1)}, bf16[256,512]{1,0:T(8,128)(2,1)}, bf16[768,128]{1,0:T(8,128)(2,1)}) custom-call(s32[2]{0:T(128)} %pad_add_fusion.where_ref, s32[4,8]{1,0:T(4,128)} %map_ref.1, bf16[4,2,128,128]{3,2,1,0:T(8,128)(2,1)} %shard_map.46.got_ref, f32[4096,128]{1,0:T(8,128)} %bitcast.8), custom_call_target="tpu_custom_call" | custom-call | tf_op jit(solution)/shard_map/pallas_call | solution.py:494
  36.3 0.0 copy-start
  36.3 22.6 %shard_map.48.blocks_ref = bf16[8192,128]{1,0:T(8,128)(2,1)} custom-call(bf16[256,128]{1,0:T(8,128)(2,1)} %get-tuple-element.15.piece_ref), custom_call_target="tpu_custom_call" | custom-call | tf_op jit(solution)/shard_map/pallas_call | solution.py:512
  59.0 0.0 all-gather.2.cloned.1.call-update
  59.0 0.0 copy-done
  59.0 0.6 collective-permute-start
  59.6 0.7 collective-permute-start.1
  60.2 0.9 collective-permute-start.2
  61.2 51.7 %shard_map.49 = (bf16[1024,1024]{1,0:T(8,128)(2,1)}, bf16[1024,128]{1,0:T(8,128)(2,1)}, f32[1024,128]{1,0:T(8,128)}) custom-call(s32[2]{0:T(128)} %pad_add_fusion.where_ref, bf16[8192,128]{1,0:T(8,128)(2,1)} %shard_map.48.blocks_ref), custom_call_target="tpu_custom_call" | custom-call | flops 8589934592 | bytes 8388608 | tf_op jit(solution)/shard_map/pallas_call | solution.py:535
  112.9 0.0 collective-permute-done
  112.9 0.0 collective-permute-done.1
  112.9 0.0 collective-permute-done.2
  112.9 1.0 pad_maximum_fusion.tops_ref
  113.9 0.0 all-gather.2.cloned.1.call-done.rows_ref
  113.9 11.1 %shard_map.50 = f32[4096,128]{1,0:T(8,128)} custom-call(s32[2]{0:T(128)} %pad_add_fusion.where_ref, bf16[1024,1024]{1,0:T(8,128)(2,1)} %get-tuple-element.19.l_ref, bf16[1024,128]{1,0:T(8,128)(2,1)} %get-tuple-element.20.z_ref, f32[1024,128]{1,0:T(8,128)} %get-tuple-element.21.own_ref, bf16[6144,128]{1,0:T(8,128)(2,1)} %all-gather.2.cloned.1.call-done.rows_ref, ...), custom_call_target="tpu_custom_call" | custom-call | tf_op jit(solution)/shard_map/pallas_call | solution.py:552
Async XLA Ops:
  6.5 107.4 %all-gather.2.cloned.1.call-start = ((), (), s32[]{:S(2)}) async-start(), calls=%async_computation | async-start | bytes 1769472 | tf_op jit(solution)/shard_map/all_gather | solution.py:528
  36.3 22.7 %copy-start = (bf16[256,512]{1,0:T(8,128)(2,1)S(1)}, bf16[256,512]{1,0:T(8,128)(2,1)}, u32[]{:S(2)}) copy-start(bf16[256,512]{1,0:T(8,128)(2,1)} %get-tuple-element.23) | copy-start | bytes 786436
  59.0 53.9 %collective-permute-start = (bf16[256,512]{1,0:T(8,128)(2,1)S(1)}, bf16[256,512]{1,0:T(8,128)(2,1)S(1)}, u32[]{:S(2)}, u32[]{:S(2)}) collective-permute-start(bf16[256,512]{1,0:T(8,128)(2,1)S(1)} %copy-done), channel_id=1, source_target_pairs={{0,8},{8,16},{16,24},{24,0},{1,9},{9,17},{17,25},{25,1},{2,10},{10... | collective-permute-start | bytes 786440 | tf_op jit(solution)/shard_map/ppermute | solution.py:460
  59.6 53.3 %collective-permute-start.1 = (bf16[256,512]{1,0:T(8,128)(2,1)S(1)}, bf16[256,512]{1,0:T(8,128)(2,1)S(1)}, u32[]{:S(2)}, u32[]{:S(2)}) collective-permute-start(bf16[256,512]{1,0:T(8,128)(2,1)S(1)} %copy-done), channel_id=1, source_target_pairs={{0,16},{8,24},{16,0},{24,8},{1,17},{9,25},{17,1},{25,9},{2,18},{10... | collective-permute-start | bytes 786440 | tf_op jit(solution)/shard_map/ppermute | solution.py:460
  60.2 52.6 %collective-permute-start.2 = (bf16[256,512]{1,0:T(8,128)(2,1)S(1)}, bf16[256,512]{1,0:T(8,128)(2,1)S(1)}, u32[]{:S(2)}, u32[]{:S(2)}) collective-permute-start(bf16[256,512]{1,0:T(8,128)(2,1)S(1)} %copy-done), channel_id=1, source_target_pairs={{0,24},{8,0},{16,8},{24,16},{1,25},{9,1},{17,9},{25,17},{2,26},{10... | collective-permute-start | bytes 786440 | tf_op jit(solution)/shard_map/ppermute | solution.py:460
Sparse Core Ops, SparseCore 0:
  59.1 43.1 all-gather.1

commit v5 on v4

--- a/solution.py
+++ b/solution.py
@@ -25,7 +25,10 @@
 
 
 def dot3(a, b, dims):
-    return dot(a[0], b[0], dims) + (dot(a[0], b[1], dims) + dot(a[1], b[0], dims))
+    (ah, al), (bh, bl) = a, b
+    left = jnp.concatenate([ah, ah, al], axis=1)
+    right = jnp.concatenate([bh, bl, bh], axis=dims[0][1][0])
+    return dot(left, right, dims)
 
 
 def factor_half(a_ref, u_ref):
@@ -60,19 +63,21 @@
             det = p00 * p11 - p01 * p01
             inv = pl.reciprocal(det, approx=True)
             inv = inv * (2.0 - det * inv)
-            c00, c01, c11 = p00 * inv, p01 * inv, p11 * inv
 
             def pivot(first, second):
-                return c11 * first - c01 * second, c00 * second - c01 * first
-
+                return p11 * first - p01 * second, p00 * second - p01 * first
+
+            raw = {}
             for m in range(j + 2, 8):
-                solved[j, m], solved[j + 1, m] = pivot(e[j, m], e[j + 1, m])
+                raw[j, m], raw[j + 1, m] = pivot(e[j, m], e[j + 1, m])
+                solved[j, m], solved[j + 1, m] = raw[j, m] * inv, raw[j + 1, m] * inv
             for m in range(j + 2, 8):
                 for k in range(m, 8):
-                    e[m, k] = e[m, k] - (e[j, m] * solved[j, k] + e[j + 1, m] * solved[j + 1, k])
+                    e[m, k] = e[m, k] - inv * (e[j, m] * raw[j, k] + e[j + 1, m] * raw[j + 1, k])
             w[j], w[j + 1] = pivot(r[j], r[j + 1])
             for m in range(j + 2, 8):
-                r[m] = r[m] - (e[j, m] * w[j] + e[j + 1, m] * w[j + 1])
+                r[m] = r[m] - inv * (e[j, m] * w[j] + e[j + 1, m] * w[j + 1])
+            w[j], w[j + 1] = w[j] * inv, w[j + 1] * inv
             d0 = lax.rsqrt(p00)
             ratio = p01 * d0 * d0
             d1 = lax.rsqrt(p11 - ratio * p01)
@@ -83,7 +88,7 @@
             break
         for j in (4, 2, 0):
             for i in (j, j + 1):
-                for k in range(j + 2, 8):
+                for k in range(7, j + 1, -1):
                     w[i] = w[i] - solved[i, k] * w[k]
         for t in range(t0 + 1, tiles):
             terms = [x[t][k] * w[k] for k in range(8)]
@@ -261,50 +266,59 @@
     return lax.rem(position - steps + count, count)
 
 
-def ring_hops(position, count, first, slot, sems):
+def ring_hops(position, count, parts, first, slot, sems, need=None):
     send, recv = sems
     half = count // 2
-    rows = first.shape[0]
+    rows = first.shape[0] // parts
     after = ring_member(lax.rem(position + 1, count), count)
     ahead = ring_member(behind(position, 1, count), count)
 
-    def hop(way, s):
+    def act(kind, way, s, u):
+        if s == half and (u < parts // 2) != (way == 0):
+            return
         to = s if way == 0 else count - s
-        source = first if s == 1 else slot(to - 1 if way == 0 else to + 1)
-        target = slot(to)
-        if s == half:
-            part = pl.ds(0, rows // 2) if way == 0 else pl.ds(rows // 2, rows // 2)
-            source, target = source.at[part], target.at[part]
-        return pltpu.make_async_remote_copy(
-            src_ref=source,
-            dst_ref=target,
-            send_sem=send.at[way, s],
-            recv_sem=recv.at[way, s],
+        before = to - 1 if way == 0 else to + 1
+        part = pl.ds(u * rows, rows)
+        copy = pltpu.make_async_remote_copy(
+            src_ref=(first if s == 1 else slot(before)).at[part],
+            dst_ref=slot(to).at[part],
+            send_sem=send.at[way, s, u],
+            recv_sem=recv.at[way, s, u],
             device_id={"front": after if way == 0 else ahead},
             device_id_type=MESH,
         )
-
-    return hop, (after, ahead)
-
-
-def ring_run(hop, half, ready):
-    for way in (0, 1):
-        hop(way, 1).start()
-    ready(0)
+        run = {"start": copy.start, "sent": copy.wait_send, "got": copy.wait_recv}[kind]
+        if need is None:
+            run()
+        else:
+            at = to if kind == "got" else before
+            pl.when(need(u, ring_member(behind(position, at, count), count)))(run)
+
+    return act, (after, ahead)
+
+
+def ring_run(act, half, parts, ready):
+    for u in range(parts):
+        for way in (0, 1):
+            act("start", way, 1, u)
+    for u in range(parts):
+        ready(0, u)
     for s in range(1, half + 1):
-        for way in (0, 1):
-            hop(way, s).wait_recv()
+        for u in range(parts):
+            for way in (0, 1):
+                act("got", way, s, u)
+                if s < half:
+                    act("start", way, s + 1, u)
+            ready(s, u)
             if s < half:
-                hop(way, s + 1).start()
-        ready(s)
-        if s < half:
-            ready(2 * half - s)
-
-
-def ring_end(hop, half):
+                ready(2 * half - s, u)
+
+
+def ring_end(act, half, parts):
     for s in range(1, half + 1):
-        for way in (0, 1):
-            hop(way, s).wait_send()
+        for u in range(parts):
+            for way in (0, 1):
+                act("sent", way, s, u)
 
 
 def greet(barrier, devices):
@@ -321,8 +335,9 @@
     size = panel_ref.shape[0]
     half = front_count // 2
     position = ring_position(front_id, front_count)
-    hop, beside = ring_hops(
-        position, front_count, panel_ref, lambda s: slots.at[s], (ring_send, ring_recv)
+    parts = ring_send.shape[2]
+    act, beside = ring_hops(
+        position, front_count, parts, panel_ref, lambda s: slots.at[s], (ring_send, ring_recv)
     )
     greet(
         pltpu.get_barrier_semaphore(),
@@ -343,7 +358,9 @@
         )
         return block, owner, turn, copy
 
-    def ready(s):
+    def ready(s, u):
+        if u + 1 < parts:
+            return
         block, owner, turn, copy = deliver(s)
         rows = panel_ref[...] if s == 0 else slots[s]
         given = blocks_ref[pl.ds(pl.multiple_of(block * size, size), size), :]
@@ -359,7 +376,7 @@
         def _():
             copy.start()
 
-    ring_run(hop, half, ready)
+    ring_run(act, half, parts, ready)
     for d in range(1, leaf_count):
         source = lax.rem(leaf_id + d, leaf_count)
         for turn in range(land.shape[1]):
@@ -375,7 +392,7 @@
     for s in range(front_count):
         _, owner, _, copy = deliver(s)
         pl.when(owner != leaf_id)(copy.wait_send)
-    ring_end(hop, half)
+    ring_end(act, half, parts)
 
 
 def corner_kernel(
@@ -383,18 +400,27 @@
     held, ring_send, ring_recv, far_send, far_recv, near_send, near_recv,
 ):
     leaf_id, front_id = lax.axis_index("leaf"), lax.axis_index("front")
-    rows = piece_ref.shape[0]
+    rows, size = piece_ref.shape
     half = front_count // 2
     chips = leaf_count // 2
     chip, core = lax.div(leaf_id, 2), lax.rem(leaf_id, 2)
     mate = leaf_id + 1 - 2 * core
     position = ring_position(front_id, front_count)
-    hop, beside = ring_hops(
+    parts = ring_send.shape[2]
+    blocks = rows // size
+    unit = rows // parts
+
+    def need(u, column, source=leaf_id):
+        return u * blocks // parts * leaf_count + source >= column
+
+    act, beside = ring_hops(
         position,
         front_count,
+        parts,
         piece_ref,
         lambda s: held.at[leaf_id, s],
         (ring_send, ring_recv),
+        need,
     )
     greet(
         pltpu.get_barrier_semaphore(),
@@ -403,54 +429,57 @@
         + [{"leaf": mate}],
     )
 
-    def far(d, s, source):
-        return pltpu.make_async_remote_copy(
-            src_ref=held.at[source, s],
-            dst_ref=held.at[source, s],
-            send_sem=far_send.at[d - 1, s],
-            recv_sem=far_recv.at[d - 1, s],
-            device_id={"leaf": 2 * lax.rem(chip + d, chips) + core},
+    def pass_on(kind, d, s, u, source, near):
+        part = held.at[source, s, pl.ds(u * unit, unit)]
+        send, recv, at = (near_send, near_recv, d) if near else (far_send, far_recv, d - 1)
+        copy = pltpu.make_async_remote_copy(
+            src_ref=part,
+            dst_ref=part,
+            send_sem=send.at[at, s, u],
+            recv_sem=recv.at[at, s, u],
+            device_id={"leaf": mate if near else 2 * lax.rem(chip + d, chips) + core},
             device_id_type=MESH,
         )
-
-    def near(d, s, source):
-        return pltpu.make_async_remote_copy(
-            src_ref=held.at[source, s],
-            dst_ref=held.at[source, s],
-            send_sem=near_send.at[d, s],
-            recv_sem=near_recv.at[d, s],
-            device_id={"leaf": mate},
-            device_id_type=MESH,
-        )
+        run = {"start": copy.start, "sent": copy.wait_send, "got": copy.wait_recv}[kind]
+        column = ring_member(behind(position, s, front_count), front_count)
+        pl.when(need(u, column, source))(run)
 
     held[leaf_id, 0] = piece_ref[...]
 
-    def ready(s):
+    def ready(s, u):
         for d in range(1, chips):
-            far(d, s, leaf_id).start()
-        near(0, s, leaf_id).start()
-
-    ring_run(hop, half, ready)
+            pass_on("start", d, s, u, leaf_id, False)
+        pass_on("start", 0, s, u, leaf_id, True)
+
+    ring_run(act, half, parts, ready)
     order = [0] + [t for s in range(1, half) for t in (s, front_count - s)] + [half]
     for s in order:
-        for d in range(1, chips):
-            source = 2 * behind(chip, d, chips) + core
-            far(d, s, source).wait_recv()
-            near(d, s, source).start()
+        for u in range(parts):
+            for d in range(1, chips):
+                source = 2 * behind(chip, d, chips) + core
+                pass_on("got", d, s, u, source, False)
+                pass_on("start", d, s, u, source, True)
     for s in order:
-        for d in range(chips):
-            near(d, s, 2 * behind(chip, d, chips) + 1 - core).wait_recv()
+        for u in range(parts):
+            for d in range(chips):
+                pass_on("got", d, s, u, 2 * behind(chip, d, chips) + 1 - core, True)
     for s in range(front_count):
         column = ring_member(behind(position, s, front_count), front_count)
         for source in range(leaf_count):
-            at = pl.multiple_of((source * front_count + column) * rows, rows)
-            out_ref[pl.ds(at, rows), :] = held[source, s]
+            for u in range(parts):
+
+                @pl.when(need(u, column, source))
+                def _():
+                    at = pl.multiple_of((source * front_count + column) * rows + u * unit, unit)
+                    out_ref[pl.ds(at, unit), :] = held[source, s, u * unit : (u + 1) * unit]
+
     for s in range(front_count):
-        for d in range(1, chips):
-            far(d, s, leaf_id).wait_send()
-        for d in range(chips):
-            near(d, s, leaf_id).wait_send()
-    ring_end(hop, half)
+        for u in range(parts):
+            for d in range(1, chips):
+                pass_on("sent", d, s, u, leaf_id, False)
+            for d in range(chips):
+                pass_on("sent", d, s, u, 2 * behind(chip, d, chips) + core, True)
+    ring_end(act, half, parts)
 
 
 def gather_by_distance(x, axis):
@@ -474,7 +503,8 @@
     params = pltpu.CompilerParams(vmem_limit_bytes=LIMIT)
     piv = child_panels.shape[2]
     half = front_count // 2
-    ring = [DMA((2, half + 1)), DMA((2, half + 1))]
+    parts = max(top, 2)
+    ring = [DMA((2, half + 1, parts))] * 2
     got = pl.pallas_call(
         functools.partial(update_kernel, leaf_count, front_count),
         out_shape=jax.ShapeDtypeStruct((children, spread, size, size), jnp.bfloat16),
@@ -518,8 +548,8 @@
         out_specs=VMEM,
         scratch_shapes=[pltpu.VMEM((leaf_count, front_count, top * size, size), jnp.bfloat16)]
         + ring
-        + [DMA((max(chips - 1, 1), front_count))] * 2
-        + [DMA((chips, front_count))] * 2,
+        + [DMA((max(chips - 1, 1), front_count, parts))] * 2
+        + [DMA((chips, front_count, parts))] * 2,
         compiler_params=pltpu.CompilerParams(
             vmem_limit_bytes=LIMIT, collective_id=1, has_side_effects=True
         ),

time: 132 us -> 124 us (0.939)
  Pallas kernels: 115 us -> 106 us
    pallas_call x1, Pallas kernels: 22.6 us -> 17.6 us  [on_device(): pl.pallas_call(functools.partial(corner_kernel, leaf_count, front_count),...]
    pallas_call x1, Pallas kernels: 51.7 us -> 48.1 us  [on_device(): pl.pallas_call(functools.partial(cholesky_kernel, corner_place), out_shap...]
where the time goes in v5:
time: 124 us; the launch traced here: 123 us
  Pallas kernels  106 us (85%)
  between operations  13.4 us (11%)
  starting transfers between devices  2.56 us (2%)
  other arithmetic  1.59 us (1%)
    pallas_call x1, Pallas kernels, on_device(): pl.pallas_call(functools.partial(cholesky_kernel, corner_place), out_shap...  48.1 us
    pallas_call x1, Pallas kernels, on_device(): pl.pallas_call(functools.partial(update_kernel, leaf_count, front_count),...  25.3 us
    pallas_call x1, Pallas kernels, on_device(): pl.pallas_call(functools.partial(corner_kernel, leaf_count, front_count),...  17.6 us
    pallas_call x1, Pallas kernels, on_device(): pl.pallas_call(functools.partial(solve_kernel, leaf_count, first), out_sh...  11.2 us
    pallas_call x1, Pallas kernels, on_device(): pl.pallas_call(functools.partial(assemble_kernel, leaf_count, front_count...  3.42 us
    ppermute x3, starting transfers between devices, gather_by_distance(): lax.ppermute(x, axis, [(i, (i + d) % count) for i in range(count)])  2.56 us
  transfers between devices with their start and end apart: 4, of which 0 were waited for; matrix products, arithmetic and copies ran while one was open for 1% of the time, Pallas kernels for 39%

profile of v5, /device:TPU:0, one launch (start us, length us, event | category | flops | bytes accessed | tf_op | source)
XLA Modules:
  0.0 123.3 jit_solution(10042647456486350845)
XLA Ops:
  6.5 0.0 all-gather.2.cloned.1.call-start
  6.5 0.6 pad_add_fusion.where_ref
  7.1 25.3 %shard_map.46.got_ref = bf16[4,2,128,128]{3,2,1,0:T(8,128)(2,1)} custom-call(bf16[128,512]{1,0:T(8,128)(2,1)} %bitcast.10, bf16[1024,128]{1,0:T(8,128)(2,1)} %bitcast.9), custom_call_target="tpu_custom_call" | custom-call | tf_op jit(solution)/shard_map/pallas_call | solution.py:508
  32.4 3.4 %shard_map.47 = (f32[4,1024,128]{2,1,0:T(8,128)}, bf16[256,128]{1,0:T(8,128)(2,1)}, bf16[256,512]{1,0:T(8,128)(2,1)}, bf16[768,128]{1,0:T(8,128)(2,1)}) custom-call(s32[2]{0:T(128)} %pad_add_fusion.where_ref, s32[4,8]{1,0:T(4,128)} %map_ref.1, bf16[4,2,128,128]{3,2,1,0:T(8,128)(2,1)} %shard_map.46.got_ref, f32[4096,128]{1,0:T(8,128)} %bitcast.8), custom_call_target="tpu_custom_call" | custom-call | tf_op jit(solution)/shard_map/pallas_call | solution.py:524
  35.9 0.0 copy-start
  35.9 17.6 %shard_map.48.blocks_ref = bf16[8192,128]{1,0:T(8,128)(2,1)} custom-call(bf16[256,128]{1,0:T(8,128)(2,1)} %get-tuple-element.15.piece_ref), custom_call_target="tpu_custom_call" | custom-call | tf_op jit(solution)/shard_map/pallas_call | solution.py:542
  53.5 0.0 all-gather.2.cloned.1.call-update
  53.5 0.0 copy-done
  53.5 1.1 collective-permute-start
  54.6 0.0 collective-permute-start.1
  54.6 1.4 %collective-permute-start.2 = (bf16[256,512]{1,0:T(8,128)(2,1)S(1)}, bf16[256,512]{1,0:T(8,128)(2,1)S(1)}, u32[]{:S(2)}, u32[]{:S(2)}) collective-permute-start(bf16[256,512]{1,0:T(8,128)(2,1)S(1)} %copy-done), channel_id=1, source_target_pairs={{0,24},{8,0},{16,8},{24,16},{1,25},{9,1},{17,9},{25,17},{2,26},{10... | collective-permute-start | bytes 786440 | tf_op jit(solution)/shard_map/ppermute | solution.py:489
  56.0 48.1 %shard_map.49 = (bf16[1024,1024]{1,0:T(8,128)(2,1)}, bf16[1024,128]{1,0:T(8,128)(2,1)}, f32[1024,128]{1,0:T(8,128)}) custom-call(s32[2]{0:T(128)} %pad_add_fusion.where_ref, bf16[8192,128]{1,0:T(8,128)(2,1)} %shard_map.48.blocks_ref), custom_call_target="tpu_custom_call" | custom-call | flops 8589934592 | bytes 8388608 | tf_op jit(solution)/shard_map/pallas_call | solution.py:565
  104.2 0.0 collective-permute-done
  104.2 0.0 collective-permute-done.1
  104.2 0.0 collective-permute-done.2
  104.2 1.0 pad_maximum_fusion.tops_ref
  105.2 0.0 all-gather.2.cloned.1.call-done.rows_ref
  105.2 11.2 %shard_map.50 = f32[4096,128]{1,0:T(8,128)} custom-call(s32[2]{0:T(128)} %pad_add_fusion.where_ref, bf16[1024,1024]{1,0:T(8,128)(2,1)} %get-tuple-element.19.l_ref, bf16[1024,128]{1,0:T(8,128)(2,1)} %get-tuple-element.20.z_ref, f32[1024,128]{1,0:T(8,128)} %get-tuple-element.21.own_ref, bf16[6144,128]{1,0:T(8,128)(2,1)} %all-gather.2.cloned.1.call-done.rows_ref, ...), custom_call_target="tpu_custom_call" | custom-call | tf_op jit(solution)/shard_map/pallas_call | solution.py:582
Async XLA Ops:
  6.5 98.7 %all-gather.2.cloned.1.call-start = ((), (), s32[]{:S(2)}) async-start(), calls=%async_computation | async-start | bytes 1769472 | tf_op jit(solution)/shard_map/all_gather | solution.py:558
  35.9 17.6 %copy-start = (bf16[256,512]{1,0:T(8,128)(2,1)S(1)}, bf16[256,512]{1,0:T(8,128)(2,1)}, u32[]{:S(2)}) copy-start(bf16[256,512]{1,0:T(8,128)(2,1)} %get-tuple-element.23) | copy-start | bytes 786436
  53.5 50.7 %collective-permute-start = (bf16[256,512]{1,0:T(8,128)(2,1)S(1)}, bf16[256,512]{1,0:T(8,128)(2,1)S(1)}, u32[]{:S(2)}, u32[]{:S(2)}) collective-permute-start(bf16[256,512]{1,0:T(8,128)(2,1)S(1)} %copy-done), channel_id=1, source_target_pairs={{0,8},{8,16},{16,24},{24,0},{1,9},{9,17},{17,25},{25,1},{2,10},{10... | collective-permute-start | bytes 786440 | tf_op jit(solution)/shard_map/ppermute | solution.py:489
  54.6 49.6 %collective-permute-start.1 = (bf16[256,512]{1,0:T(8,128)(2,1)S(1)}, bf16[256,512]{1,0:T(8,128)(2,1)S(1)}, u32[]{:S(2)}, u32[]{:S(2)}) collective-permute-start(bf16[256,512]{1,0:T(8,128)(2,1)S(1)} %copy-done), channel_id=1, source_target_pairs={{0,16},{8,24},{16,0},{24,8},{1,17},{9,25},{17,1},{25,9},{2,18},{10... | collective-permute-start | bytes 786440 | tf_op jit(solution)/shard_map/ppermute | solution.py:489
  54.6 49.6 %collective-permute-start.2 = (bf16[256,512]{1,0:T(8,128)(2,1)S(1)}, bf16[256,512]{1,0:T(8,128)(2,1)S(1)}, u32[]{:S(2)}, u32[]{:S(2)}) collective-permute-start(bf16[256,512]{1,0:T(8,128)(2,1)S(1)} %copy-done), channel_id=1, source_target_pairs={{0,24},{8,0},{16,8},{24,16},{1,25},{9,1},{17,9},{25,17},{2,26},{10... | collective-permute-start | bytes 786440 | tf_op jit(solution)/shard_map/ppermute | solution.py:489
Sparse Core Ops, SparseCore 0:
  53.6 45.7 all-gather.1

commit v6 on v5

--- a/solution.py
+++ b/solution.py
@@ -31,33 +31,33 @@
     return dot(left, right, dims)
 
 
-def factor_half(a_ref, u_ref):
-    size, width = a_ref.shape
+def factor_block(d_ref, u_ref, z_ref):
+    size = d_ref.shape[0]
     tiles = size // 8
-    sub = lax.broadcasted_iota(jnp.int32, (8, width), 0)
-    lane = lax.broadcasted_iota(jnp.int32, (8, width), 1)
-    a = [
-        jnp.where(
-            lane < size,
-            a_ref[8 * t : 8 * t + 8, :],
-            jnp.where(lane == sub + (size + 8 * t), 1.0, 0.0),
+    sub = lax.broadcasted_iota(jnp.int32, (8, size), 0)
+    lane = lax.broadcasted_iota(jnp.int32, (8, size), 1)
+    a = [d_ref[8 * t : 8 * t + 8, :] for t in range(tiles)]
+    z = [jnp.where(lane == sub + 8 * t, 1.0, 0.0).astype(jnp.float32) for t in range(tiles)]
+
+    def row(tile, s):
+        return jnp.broadcast_to(tile[s : s + 1, :], (8, size))
+
+    def column(tile, j):
+        return jnp.broadcast_to(tile[:, j : j + 1], (8, size))
+
+    def total(x, w):
+        terms = [x[k] * w[k] for k in range(8)]
+        return ((terms[0] + terms[1]) + (terms[2] + terms[3])) + (
+            (terms[4] + terms[5]) + (terms[6] + terms[7])
         )
-        for t in range(tiles)
-    ]
-
-    def row(tile, s):
-        return jnp.broadcast_to(tile[s : s + 1, :], (8, width))
-
-    def column(tile, j):
-        return jnp.broadcast_to(tile[:, j : j + 1], (8, width))
 
     for t0 in range(tiles):
         base = 8 * t0
         spread = [column(a[t0], base + k) for k in range(8)]
         e = {(m, k): row(spread[k], m) for k in range(8) for m in range(k + 1)}
-        r = [row(a[t0], m) for m in range(8)]
+        sides = [[row(a[t0], m) for m in range(8)], [row(z[t0], m) for m in range(8)]]
         x = {t: [column(a[t], base + k) for k in range(8)] for t in range(t0 + 1, tiles)}
-        w, solved = [None] * 8, {}
+        both, solved = [[None] * 8, [None] * 8], {}
         for j in range(0, 8, 2):
             p00, p01, p11 = e[j, j], e[j, j + 1], e[j + 1, j + 1]
             det = p00 * p11 - p01 * p01
@@ -74,56 +74,31 @@
             for m in range(j + 2, 8):
                 for k in range(m, 8):
                     e[m, k] = e[m, k] - inv * (e[j, m] * raw[j, k] + e[j + 1, m] * raw[j + 1, k])
-            w[j], w[j + 1] = pivot(r[j], r[j + 1])
-            for m in range(j + 2, 8):
-                r[m] = r[m] - inv * (e[j, m] * w[j] + e[j + 1, m] * w[j + 1])
-            w[j], w[j + 1] = w[j] * inv, w[j + 1] * inv
             d0 = lax.rsqrt(p00)
             ratio = p01 * d0 * d0
             d1 = lax.rsqrt(p11 - ratio * p01)
             at = base + j
-            u_ref[at : at + 1, :] = (r[j] * d0)[:1]
-            u_ref[at + 1 : at + 2, :] = ((r[j + 1] - ratio * r[j]) * d1)[:1]
+            for r, w, out_ref in zip(sides, both, (u_ref, z_ref)):
+                first, second = pivot(r[j], r[j + 1])
+                w[j], w[j + 1] = first * inv, second * inv
+                for m in range(j + 2, 8):
+                    r[m] = r[m] - (e[j, m] * w[j] + e[j + 1, m] * w[j + 1])
+                out_ref[at : at + 1, :] = (r[j] * d0)[:1]
+                out_ref[at + 1 : at + 2, :] = ((r[j + 1] - ratio * r[j]) * d1)[:1]
         if t0 + 1 == tiles:
             break
-        for j in (4, 2, 0):
-            for i in (j, j + 1):
-                for k in range(7, j + 1, -1):
-                    w[i] = w[i] - solved[i, k] * w[k]
+        for w in both:
+            for j in (4, 2, 0):
+                for i in (j, j + 1):
+                    for k in range(7, j + 1, -1):
+                        w[i] = w[i] - solved[i, k] * w[k]
         for t in range(t0 + 1, tiles):
-            terms = [x[t][k] * w[k] for k in range(8)]
-            a[t] = a[t] - (
-                ((terms[0] + terms[1]) + (terms[2] + terms[3]))
-                + ((terms[4] + terms[5]) + (terms[6] + terms[7]))
-            )
-
-
-def factor_block(d_ref, l_ref, z_ref, h_ref, u_ref):
-    size = d_ref.shape[0]
-    half = size // 2
-    keep = lax.broadcasted_iota(jnp.int32, (half, half), 0) >= lax.broadcasted_iota(
-        jnp.int32, (half, half), 1
-    )
-    empty = jnp.zeros((half, half), jnp.float32)
-    factor_half(d_ref.at[:half, :], u_ref)
-    z1 = halves(u_ref[:, half:])
-    l_ref[:half, :half] = jnp.where(keep, u_ref[:, :half].T, 0.0)
-    z_ref[:half, :half] = u_ref[:, half:]
-    l21 = dot3(halves(d_ref[half:, :half]), z1, NT)
-    part = halves(l21)
-    h_ref[:, :half] = d_ref[half:, half:] - dot3(part, part, NT)
-    l_ref[half:, :half] = l21
-    l_ref[:half, half:] = empty
-    z_ref[:half, half:] = empty
-    cross = halves(dot3(part, z1, NN))
-    factor_half(h_ref, u_ref)
-    l_ref[half:, half:] = jnp.where(keep, u_ref[:, :half].T, 0.0)
-    z_ref[half:, half:] = u_ref[:, half:]
-    z_ref[half:, :half] = -dot3(halves(u_ref[:, half:]), cross, NN)
+            a[t] = a[t] - total(x[t], both[0])
+            z[t] = z[t] - total(x[t], both[1])
 
 
 def cholesky_kernel(
-    place, where_ref, blocks_ref, l_ref, z_ref, own_ref, a_ref, d_ref, f_ref, i_ref, h_ref, u_ref
+    place, where_ref, blocks_ref, l_ref, z_ref, own_ref, a_ref, d_ref, u_ref, i_ref
 ):
     size = blocks_ref.shape[1]
     for j in range(KS):
@@ -133,17 +108,19 @@
                 at * size : (at + 1) * size, :
             ].astype(jnp.float32)
     d_ref[...] = a_ref[:size, :size]
-    h_ref[...] = jnp.zeros_like(h_ref)
+    keep = lax.broadcasted_iota(jnp.int32, (size, size), 0) >= lax.broadcasted_iota(
+        jnp.int32, (size, size), 1
+    )
 
     def step(k, carry):
-        factor_block(d_ref, f_ref, i_ref, h_ref, u_ref)
+        factor_block(d_ref, u_ref, i_ref)
         begin = pl.multiple_of(k * size, size)
         z_ref[pl.ds(begin, size), :] = i_ref[...].astype(z_ref.dtype)
 
         @pl.when(where_ref[1] == k)
         def _():
             own_ref[...] = jnp.zeros_like(own_ref)
-            own_ref[pl.ds(begin, size), :] = f_ref[...]
+            own_ref[pl.ds(begin, size), :] = jnp.where(keep, u_ref[...].T, 0.0)
 
         for now in range(KS - 1):
 
@@ -151,8 +128,8 @@
             def _():
                 low, high = now * size, (now + 1) * size
                 panel = dot3(halves(a_ref[high:, low:high]), halves(i_ref[...]), NT)
-                parts = halves(panel)
-                l_ref[high:, low:high] = parts[0]
+                rounded = panel.astype(jnp.bfloat16)
+                l_ref[high:, low:high] = rounded
 
                 @pl.when(where_ref[1] == now)
                 def _():
@@ -160,10 +137,10 @@
 
                 for j in range(now + 1, KS):
                     skip = (j - now - 1) * size
-                    left = tuple(x[skip:] for x in parts)
-                    right = tuple(x[skip : skip + size] for x in parts)
                     at = j * size
-                    fresh = a_ref[at:, at : at + size] - dot3(left, right, NT)
+                    fresh = a_ref[at:, at : at + size] - dot(
+                        rounded[skip:], rounded[skip : skip + size], NT
+                    )
                     if j == now + 1:
                         d_ref[...] = fresh[:size]
                     a_ref[at:, at : at + size] = fresh
@@ -572,8 +549,7 @@
         in_specs=[SMEM, VMEM],
         out_specs=[VMEM] * 3,
         scratch_shapes=[pltpu.VMEM((width, width), jnp.float32)]
-        + [pltpu.VMEM((size, size), jnp.float32)] * 3
-        + [pltpu.VMEM((size // 2, size), jnp.float32)] * 2,
+        + [pltpu.VMEM((size, size), jnp.float32)] * 3,
         compiler_params=params,
         cost_estimate=pl.CostEstimate(
             flops=8 * width**3, bytes_accessed=8 * width * width, transcendentals=0

time: 124 us -> 118 us (0.952)
  Pallas kernels: 106 us -> 99.9 us
    pallas_call x1, Pallas kernels: 48.1 us -> 42.4 us  [on_device(): pl.pallas_call(functools.partial(cholesky_kernel, corner_place), out_shap...]
  transfers between devices with their start and end apart: 4 -> 4, of which waited for: 0 -> 0; matrix products, arithmetic and copies ran while one was open for 1% -> 1% of each run, Pallas kernels for 39% -> 36%
where the time goes in v6:
time: 118 us
  Pallas kernels  99.9 us (85%)
  between operations  13.4 us (11%)
  starting transfers between devices  2.56 us (2%)
  other arithmetic  1.59 us (1%)
    pallas_call x1, Pallas kernels, on_device(): pl.pallas_call(functools.partial(cholesky_kernel, corner_place), out_shap...  42.4 us
    pallas_call x1, Pallas kernels, on_device(): pl.pallas_call(functools.partial(update_kernel, leaf_count, front_count),...  25.3 us
    pallas_call x1, Pallas kernels, on_device(): pl.pallas_call(functools.partial(corner_kernel, leaf_count, front_count),...  17.6 us
    pallas_call x1, Pallas kernels, on_device(): pl.pallas_call(functools.partial(solve_kernel, leaf_count, first), out_sh...  11.2 us
    pallas_call x1, Pallas kernels, on_device(): pl.pallas_call(functools.partial(assemble_kernel, leaf_count, front_count...  3.42 us
    ppermute x3, starting transfers between devices, gather_by_distance(): lax.ppermute(x, axis, [(i, (i + d) % count) for i in range(count)])  2.56 us
  transfers between devices with their start and end apart: 4, of which 0 were waited for; matrix products, arithmetic and copies ran while one was open for 1% of the time, Pallas kernels for 36%

profile of v6, /device:TPU:0, one launch (start us, length us, event | category | flops | bytes accessed | tf_op | source)
XLA Modules:
  0.0 117.5 jit_solution(9764010711432236096)
XLA Ops:
  6.5 0.0 all-gather.2.cloned.1.call-start
  6.5 0.6 pad_add_fusion.where_ref
  7.1 25.3 %shard_map.46.got_ref = bf16[4,2,128,128]{3,2,1,0:T(8,128)(2,1)} custom-call(bf16[128,512]{1,0:T(8,128)(2,1)} %bitcast.10, bf16[1024,128]{1,0:T(8,128)(2,1)} %bitcast.9), custom_call_target="tpu_custom_call" | custom-call | tf_op jit(solution)/shard_map/pallas_call | solution.py:485
  32.4 3.4 %shard_map.47 = (f32[4,1024,128]{2,1,0:T(8,128)}, bf16[256,128]{1,0:T(8,128)(2,1)}, bf16[256,512]{1,0:T(8,128)(2,1)}, bf16[768,128]{1,0:T(8,128)(2,1)}) custom-call(s32[2]{0:T(128)} %pad_add_fusion.where_ref, s32[4,8]{1,0:T(4,128)} %map_ref.1, bf16[4,2,128,128]{3,2,1,0:T(8,128)(2,1)} %shard_map.46.got_ref, f32[4096,128]{1,0:T(8,128)} %bitcast.8), custom_call_target="tpu_custom_call" | custom-call | tf_op jit(solution)/shard_map/pallas_call | solution.py:501
  35.9 0.0 copy-start
  35.9 17.6 %shard_map.48.blocks_ref = bf16[8192,128]{1,0:T(8,128)(2,1)} custom-call(bf16[256,128]{1,0:T(8,128)(2,1)} %get-tuple-element.15.piece_ref), custom_call_target="tpu_custom_call" | custom-call | tf_op jit(solution)/shard_map/pallas_call | solution.py:519
  53.5 0.0 all-gather.2.cloned.1.call-update
  53.5 0.0 copy-done
  53.5 1.1 collective-permute-start
  54.6 0.0 collective-permute-start.1
  54.6 1.4 %collective-permute-start.2 = (bf16[256,512]{1,0:T(8,128)(2,1)S(1)}, bf16[256,512]{1,0:T(8,128)(2,1)S(1)}, u32[]{:S(2)}, u32[]{:S(2)}) collective-permute-start(bf16[256,512]{1,0:T(8,128)(2,1)S(1)} %copy-done), channel_id=1, source_target_pairs={{0,24},{8,0},{16,8},{24,16},{1,25},{9,1},{17,9},{25,17},{2,26},{10... | collective-permute-start | bytes 786440 | tf_op jit(solution)/shard_map/ppermute | solution.py:466
  56.0 42.4 %shard_map.49 = (bf16[1024,1024]{1,0:T(8,128)(2,1)}, bf16[1024,128]{1,0:T(8,128)(2,1)}, f32[1024,128]{1,0:T(8,128)}) custom-call(s32[2]{0:T(128)} %pad_add_fusion.where_ref, bf16[8192,128]{1,0:T(8,128)(2,1)} %shard_map.48.blocks_ref), custom_call_target="tpu_custom_call" | custom-call | flops 8589934592 | bytes 8388608 | tf_op jit(solution)/shard_map/pallas_call | solution.py:542
  98.5 0.0 collective-permute-done
  98.5 0.0 collective-permute-done.1
  98.5 0.0 collective-permute-done.2
  98.5 1.0 pad_maximum_fusion.tops_ref
  99.5 0.0 all-gather.2.cloned.1.call-done.rows_ref
  99.5 11.2 %shard_map.50 = f32[4096,128]{1,0:T(8,128)} custom-call(s32[2]{0:T(128)} %pad_add_fusion.where_ref, bf16[1024,1024]{1,0:T(8,128)(2,1)} %get-tuple-element.19.l_ref, bf16[1024,128]{1,0:T(8,128)(2,1)} %get-tuple-element.20.z_ref, f32[1024,128]{1,0:T(8,128)} %get-tuple-element.21.own_ref, bf16[6144,128]{1,0:T(8,128)(2,1)} %all-gather.2.cloned.1.call-done.rows_ref, ...), custom_call_target="tpu_custom_call" | custom-call | tf_op jit(solution)/shard_map/pallas_call | solution.py:558
Async XLA Ops:
  6.5 93.0 %all-gather.2.cloned.1.call-start = ((), (), s32[]{:S(2)}) async-start(), calls=%async_computation | async-start | bytes 1769472 | tf_op jit(solution)/shard_map/all_gather | solution.py:535
  35.9 17.6 %copy-start = (bf16[256,512]{1,0:T(8,128)(2,1)S(1)}, bf16[256,512]{1,0:T(8,128)(2,1)}, u32[]{:S(2)}) copy-start(bf16[256,512]{1,0:T(8,128)(2,1)} %get-tuple-element.23) | copy-start | bytes 786436
  53.5 45.0 %collective-permute-start = (bf16[256,512]{1,0:T(8,128)(2,1)S(1)}, bf16[256,512]{1,0:T(8,128)(2,1)S(1)}, u32[]{:S(2)}, u32[]{:S(2)}) collective-permute-start(bf16[256,512]{1,0:T(8,128)(2,1)S(1)} %copy-done), channel_id=1, source_target_pairs={{0,8},{8,16},{16,24},{24,0},{1,9},{9,17},{17,25},{25,1},{2,10},{10... | collective-permute-start | bytes 786440 | tf_op jit(solution)/shard_map/ppermute | solution.py:466
  54.6 43.9 %collective-permute-start.1 = (bf16[256,512]{1,0:T(8,128)(2,1)S(1)}, bf16[256,512]{1,0:T(8,128)(2,1)S(1)}, u32[]{:S(2)}, u32[]{:S(2)}) collective-permute-start(bf16[256,512]{1,0:T(8,128)(2,1)S(1)} %copy-done), channel_id=1, source_target_pairs={{0,16},{8,24},{16,0},{24,8},{1,17},{9,25},{17,1},{25,9},{2,18},{10... | collective-permute-start | bytes 786440 | tf_op jit(solution)/shard_map/ppermute | solution.py:466
  54.6 43.9 %collective-permute-start.2 = (bf16[256,512]{1,0:T(8,128)(2,1)S(1)}, bf16[256,512]{1,0:T(8,128)(2,1)S(1)}, u32[]{:S(2)}, u32[]{:S(2)}) collective-permute-start(bf16[256,512]{1,0:T(8,128)(2,1)S(1)} %copy-done), channel_id=1, source_target_pairs={{0,24},{8,0},{16,8},{24,16},{1,25},{9,1},{17,9},{25,17},{2,26},{10... | collective-permute-start | bytes 786440 | tf_op jit(solution)/shard_map/ppermute | solution.py:466
Sparse Core Ops, SparseCore 0:
  53.6 45.7 all-gather.1
